TPU v7x, 256 devices: a whole 4x4x8 slice. The times are simulated.
256 devices in a mesh: dp: 4 (over z_hi, core), mp: 64 (over y, z_lo, x).
Axes of the slice: x: 4, y: 4, z: 8 (z_hi: 2, z_lo: 4; z = z_hi * 4 + z_lo), core: 2. Of those that a mesh axis runs over, the one named last changes fastest.
Arguments:
- tokens: bfloat16 [1024, 6144], P(('dp', 'mp')), may hold values from -6 to 6
- cotangent: bfloat16 [1024, 6144], P(('dp', 'mp')), may hold values from -6 to 6
- ln_gain: float32 [6144], replicated, may hold values from 0.5 to 1.5
- qk_gain: float32 [2, 128], replicated, may hold values from 0.5 to 6
- w_qkv: bfloat16 [3, 4096, 6144], P(None, 'mp'), may hold values from -0.05103104 to 0.05103104
- w_mlp_in: bfloat16 [16384, 6144], P('mp'), may hold values from -0.078125 to 0.078125
- w_attn_out: bfloat16 [4096, 6144], P('mp'), may hold values from -0.0390625 to 0.0390625
- w_mlp_out: bfloat16 [16384, 6144], P('mp'), may hold values from -0.0390625 to 0.0390625
Outputs:
- output: bfloat16 [1024, 6144], P(('dp', 'mp'))
- d_tokens: bfloat16 [1024, 6144], P(('dp', 'mp'))
- g_ln_gain: float32 [6144], replicated
- g_qk_gain: float32 [2, 128], replicated
- g_w_qkv: bfloat16 [3, 4096, 6144], P(None, 'mp', 'dp')
- g_w_mlp_in: bfloat16 [16384, 6144], P('mp', 'dp')
- g_w_attn_out: bfloat16 [4096, 6144], P('mp', 'dp')
- g_w_mlp_out: bfloat16 [16384, 6144], P('mp', 'dp')
All inputs are finite; a program needn't handle non-finite values.
Results may differ from a plain program's by a relative error of at most 0.034.
The roundings to bfloat16 on the way count: a program that leaves them out, or rounds other values in their place, can miss the bound.
Values may be sent and summed in bfloat16 or wider, within the bound.
No kernel may reach another device: no remote copies, remote signals or barrier semaphores. Data moves between devices by JAX's collectives and lax.ppermute only.
A program may use at most 128 MiB of HBM per device.

v0:
```python
import functools
import math

import jax
import jax.numpy as jnp
from jax import lax
from jax.experimental import pallas as pl
from jax.experimental.pallas import tpu as pltpu
from jax.sharding import PartitionSpec as P

D = 6144
HD = 128
ROWS = 256
QUARTER = D // 4
EPS = 1e-06
X, Z, Y = 1, 4, 16
BF16 = jnp.bfloat16
F32 = jnp.float32
VMEM = pl.BlockSpec(memory_space=pltpu.VMEM)
SMEM = pl.BlockSpec(memory_space=pltpu.SMEM)
ANY = pl.BlockSpec(memory_space=pl.ANY)
PARAMS = pltpu.CompilerParams(vmem_limit_bytes=48 * 1024 * 1024)


def shape(*dims, dtype=BF16):
    return jax.ShapeDtypeStruct(dims, dtype)


def swapped(block, axis, mask):
    count = lax.axis_size(axis)
    return lax.ppermute(block, axis, [(low, low ^ mask) for low in range(count)])


def pieces(block, unit):
    return [block] + [swapped(block, "mp", step * unit) for step in (1, 2, 3)]


def exchanged(blocks, unit):
    return [blocks[0]] + [swapped(blocks[step], "mp", step * unit) for step in (1, 2, 3)]


def two_steps(block):
    half = block.shape[1] // 2
    opposite = swapped(block, "mp", 2 * X)
    pair = jnp.concatenate([block, opposite], 0)
    return [
        block,
        opposite,
        swapped(pair[:, :half], "mp", X),
        swapped(pair[:, half:], "mp", 3 * X),
    ]


def total(blocks):
    first, second, third, fourth = (block.astype(F32) for block in blocks)
    return (first + second) + (third + fourth)


def two_parts(values):
    high = values.astype(BF16)
    return high, (values - high.astype(F32)).astype(BF16)


def standardize(values):
    average = jnp.mean(values, -1, keepdims=True)
    centered = values - average
    inv_std = lax.rsqrt(jnp.mean(centered * centered, -1, keepdims=True) + EPS)
    return (centered * inv_std, inv_std)


def norm_back(gradient, scaled, inv_std, gain_row):
    weighted = gradient * gain_row
    return inv_std * (
        weighted
        - jnp.mean(weighted, -1, keepdims=True)
        - scaled * jnp.mean(weighted * scaled, -1, keepdims=True)
    )


def times_rows(left, weight):
    return lax.dot_general(left, weight, (((1,), (1,)), ((), ())), preferred_element_type=F32)


def row_contract(left, right):
    return lax.dot_general(left, right, (((0,), (0,)), ((), ())), preferred_element_type=F32)


def dot(left, right):
    return jnp.dot(left, right, preferred_element_type=F32)


def start_kernel(tokens, cotangent, gain, out):
    scaled, _ = standardize(tokens[...].astype(F32))
    both = jnp.concatenate([scaled * gain[...], cotangent[...].astype(F32)], 0)
    out[...] = both.astype(BF16)


def start(tokens, cotangent, gain):
    return pl.pallas_call(
        start_kernel,
        out_shape=shape(8, D),
        in_specs=[VMEM] * 3,
        out_specs=VMEM,
        compiler_params=PARAMS,
    )(tokens, cotangent, gain)


def apart_kernel(place, *refs):
    n_out, c_out, away = refs[4:]
    left = pl.multiple_of((1 - place[0]) * (D // 2), D // 2)
    for part, (out, rows) in enumerate(((n_out, slice(0, 16)), (c_out, slice(16, 32)))):
        half = slice(4 * part, 4 * part + 4)
        blocks = [ref[...].astype(F32)[half] for ref in refs[:4]]
        whole = jnp.concatenate(blocks, 0).astype(BF16)
        for at in range(out.shape[0] // 16):
            out[16 * at : 16 * at + 16, :] = whole
        away[rows, :] = out[0:16, pl.ds(left, D // 2)]


def apart(place, parts):
    return pl.pallas_call(
        apart_kernel,
        out_shape=[shape(16, D), shape(64, D), shape(32, D // 2)],
        in_specs=[SMEM] + [VMEM] * 4,
        out_specs=[VMEM] * 3,
        compiler_params=PARAMS,
    )(place, *parts)


def join_kernel(*refs):
    for at in range(4):
        refs[4][16 * at : 16 * at + 16, :] = refs[at][...]


def join(parts):
    return pl.pallas_call(
        join_kernel,
        out_shape=shape(64, D),
        in_specs=[VMEM] * 4,
        out_specs=VMEM,
        compiler_params=PARAMS,
    )(*parts)


def n_moves(parts, target):
    return [(parts[at], target.at[pl.ds(64 * at, 64)]) for at in range(4)]


def c_moves(place, parts, target):
    half = parts[0].shape[1] // 2
    left, right = pl.ds(0, half), pl.ds(half, half)
    moves = []
    for up in range(4):
        first = pl.multiple_of(place[23 + up], 16)
        rows, lower = pl.ds(first, 16), pl.ds(64 + first, 16)
        spots = [pl.ds(64 * up + 16 * at, 16) for at in range(4)]
        moves += [
            (parts[0].at[rows], target.at[spots[0]]),
            (parts[1].at[rows], target.at[spots[2]]),
            (parts[2].at[rows], target.at[spots[1], left]),
            (parts[2].at[lower], target.at[spots[3], left]),
            (parts[3].at[rows], target.at[spots[3], right]),
            (parts[3].at[lower], target.at[spots[1], right]),
        ]
    return moves


def first_kernel(*refs):
    place, n_parts, c_parts, weights = refs[0], refs[1:5], refs[5:9], refs[9:11]
    n_out, c_out, qk_ref, vd_ref = refs[11:15]
    n_all, c_all, wq, wo, sems = refs[15:]
    copies = []

    def begin(source, target):
        copy = pltpu.make_async_copy(source, target, sems.at[len(copies)])
        copy.start()
        copies.append(copy)
        return copy

    n_in = [begin(*move) for move in n_moves(n_parts, n_all)]
    wq_in = begin(weights[0], wq)
    c_in = [begin(*move) for move in c_moves(place, c_parts, c_all)]
    wo_in = begin(weights[1], wo)
    for copy in n_in:
        copy.wait()
    wq_in.wait()
    n_done = begin(n_all, n_out)
    cols = wo.shape[0]
    projected = jnp.zeros((ROWS, 3 * cols), F32)
    for at in range(4):
        span = slice(QUARTER * at, QUARTER * at + QUARTER)
        projected += times_rows(n_all[:, span], wq[:, span])
    qk_ref[...] = projected[:, : 2 * cols]
    for copy in c_in:
        copy.wait()
    wo_in.wait()
    c_done = begin(c_all, c_out)
    d_context = jnp.zeros((ROWS, cols), F32)
    for at in range(4):
        span = slice(QUARTER * at, QUARTER * at + QUARTER)
        d_context += times_rows(c_all[:, span], wo[:, span])
    vd_ref[...] = jnp.concatenate([projected[:, 2 * cols :], d_context], 1).astype(BF16)
    n_done.wait()
    c_done.wait()


def first(place, n_parts, c_parts, w_flat, w_out):
    cols = w_out.shape[0]
    return pl.pallas_call(
        first_kernel,
        out_shape=[
            shape(ROWS, D),
            shape(ROWS, D),
            shape(ROWS, 2 * cols, dtype=F32),
            shape(ROWS, 2 * cols),
        ],
        in_specs=[SMEM] + [ANY] * 10,
        out_specs=[ANY, ANY, VMEM, VMEM],
        scratch_shapes=[
            pltpu.VMEM((ROWS, D), BF16),
            pltpu.VMEM((ROWS, D), BF16),
            pltpu.VMEM((3 * cols, D), BF16),
            pltpu.VMEM((cols, D), BF16),
            pltpu.SemaphoreType.DMA((32,)),
        ],
        compiler_params=PARAMS,
    )(place, *n_parts, *c_parts, w_flat, w_out)


def hidden_kernel(n_ref, c_ref, win, wout, out, *scratch):
    n_all, c_all, w_in, w_out, sems = scratch
    loads = []
    for at in range(4):
        span = pl.ds(QUARTER * at, QUARTER)
        pairs = ((n_ref, n_all), (win, w_in), (c_ref, c_all), (wout, w_out))
        for which, (source, target) in enumerate(pairs):
            copy = pltpu.make_async_copy(
                source.at[:, span], target.at[:, span], sems.at[at, which]
            )
            copy.start()
            loads.append(copy)
    units = w_in.shape[0]
    hidden = jnp.zeros((ROWS, units), F32)
    d_act = jnp.zeros((ROWS, units), F32)
    for at in range(4):
        for copy in loads[4 * at : 4 * at + 4]:
            copy.wait()
        span = slice(QUARTER * at, QUARTER * at + QUARTER)
        hidden += times_rows(n_all[:, span], w_in[:, span])
        d_act += times_rows(c_all[:, span], w_out[:, span])
    cdf = 0.5 * (1.0 + lax.erf(hidden * 0.7071067811865476))
    pdf = jnp.exp(-0.5 * hidden * hidden) * 0.3989422804014327
    out[:, units:] = (hidden * cdf).astype(BF16)
    out[:, :units] = (d_act.astype(BF16).astype(F32) * (cdf + hidden * pdf)).astype(BF16)


def hidden(n_all, c_all, w_in, w_out):
    units = w_in.shape[0]
    return pl.pallas_call(
        hidden_kernel,
        out_shape=shape(ROWS, 2 * units),
        in_specs=[ANY] * 4,
        out_specs=VMEM,
        scratch_shapes=[
            pltpu.VMEM((ROWS, D), BF16),
            pltpu.VMEM((ROWS, D), BF16),
            pltpu.VMEM((units, D), BF16),
            pltpu.VMEM((units, D), BF16),
            pltpu.SemaphoreType.DMA((4, 4)),
        ],
        compiler_params=PARAMS,
    )(n_all, c_all, w_in, w_out)


def head_kernel(place, qk_own, qk_peer, vd_own, vd_peer, gains, ad, out, gain_ref):
    cols = HD // 2

    def whole(own, peer, left):
        other = jnp.concatenate(
            [peer[16 * (at ^ 1) : 16 * (at ^ 1) + 16, :] for at in range(ROWS // 16)], 0
        )
        return jnp.concatenate(
            [own[:, left : left + cols], other[:, left : left + cols]], 1
        )

    query, key = whole(qk_own, qk_peer, 0), whole(qk_own, qk_peer, cols)
    values, d_ctx = whole(vd_own, vd_peer, 0), whole(vd_own, vd_peer, cols)
    q_gain, k_gain = gains[0:1, :], gains[1:2, :]
    q_scaled, q_inv = standardize(query)
    k_scaled, k_inv = standardize(key)
    q_normed = (q_scaled * q_gain).astype(BF16)
    k_normed = (k_scaled * k_gain).astype(BF16)
    scores = times_rows(q_normed, k_normed) * (1.0 / math.sqrt(HD))
    grown = jnp.exp(scores - jnp.max(scores, -1, keepdims=True))
    probs = (grown / jnp.sum(grown, -1, keepdims=True)).astype(BF16)
    context = dot(probs, values)[:, :cols]
    d_probs = times_rows(d_ctx, values)
    probs_f = probs.astype(F32)
    centered = d_probs - jnp.sum(probs_f * d_probs, -1, keepdims=True)
    d_scores = (probs_f * centered * (1.0 / math.sqrt(HD))).astype(BF16)
    d_values = row_contract(probs, d_ctx)
    d_qn = dot(d_scores, k_normed)
    d_kn = row_contract(d_scores, q_normed)
    d_query = norm_back(d_qn, q_scaled, q_inv, q_gain)
    d_key = norm_back(d_kn, k_scaled, k_inv, k_gain)
    out[:, :HD] = jnp.concatenate([d_query[:, :cols], d_key[:, :cols]], 1).astype(BF16)
    out[:, HD : 2 * HD] = jnp.concatenate([d_values[:, :cols], context], 1).astype(BF16)
    out[:, 2 * HD :] = ad[...]
    for row, terms in enumerate((d_qn * q_scaled, d_kn * k_scaled)):
        mine = jnp.sum(terms, 0, keepdims=True)[:, :cols]
        none = jnp.zeros_like(mine)
        even = jnp.concatenate([mine, none], 1)
        odd = jnp.concatenate([none, mine], 1)
        gain_ref[row : row + 1, :] = jnp.where(place[2] == 0, even, odd)


def head(place, qk_own, qk_peer, vd_own, vd_peer, gains, ad):
    return pl.pallas_call(
        head_kernel,
        out_shape=[shape(ROWS, 2 * HD + ad.shape[1]), shape(2, HD, dtype=F32)],
        in_specs=[SMEM] + [VMEM] * 6,
        out_specs=[VMEM] * 2,
        compiler_params=PARAMS,
    )(place, qk_own, qk_peer, vd_own, vd_peer, gains, ad)


SLAB = 1024
STEPS = D // SLAB


def back_kernel(acts, w_ao, w_mo, w_qkv, w_mi, n_ref, gain, gain_part, *outs):
    mix_outs, kept, opposite, near_left, near_right, sums = outs[:4], *outs[4:]
    at = pl.program_id(0)
    ins, units, heads = w_qkv.shape[0], w_mi.shape[0], 2 * HD
    d_norm = dot(acts[:, :ins], w_qkv[...]) + dot(acts[:, heads : heads + units], w_mi[...])
    part = jnp.sum(d_norm * n_ref[...].astype(F32), 0, keepdims=True) / gain[...]

    @pl.when(at == 0)
    def _():
        sums[48:64, :] = jnp.zeros((16, 128), F32)
        sums[48:50, :] = gain_part[...]

    for k in range(SLAB // 128):
        sums[pl.ds(SLAB // 128 * at + k, 1), :] = part[:, 128 * k : 128 * k + 128]

    chunks = [
        jnp.concatenate(
            [d_norm[64 * up + 16 * k : 64 * up + 16 * k + 16] for up in range(4)], 0
        ).astype(BF16)
        for k in range(4)
    ]
    kept[...] = chunks[0]
    opposite[...] = chunks[2]

    @pl.when(at < STEPS // 2)
    def _():
        near_left[:64, :] = chunks[1]
        near_left[64:, :] = chunks[3]

    @pl.when(at >= STEPS // 2)
    def _():
        near_right[:64, :] = chunks[3]
        near_right[64:, :] = chunks[1]

    mixed = dot(acts[:, ins:heads], w_ao[...]) + dot(acts[:, heads + units :], w_mo[...])
    for k in range(4):
        mix_outs[k][...] = mixed[64 * k : 64 * k + 64].astype(BF16)


def back(acts, w_ao, w_mo, w_qkv, w_mi, n_all, ln_gain, gain_part):
    larges = (w_ao, w_mo, w_qkv, w_mi, n_all, ln_gain)
    half = STEPS // 2
    return pl.pallas_call(
        back_kernel,
        grid=(STEPS,),
        out_shape=[shape(64, D)] * 6
        + [shape(128, D // 2)] * 2
        + [shape(64, 128, dtype=F32)],
        in_specs=[pl.BlockSpec(acts.shape, lambda at: (0, 0))]
        + [pl.BlockSpec((one.shape[0], SLAB), lambda at: (0, at)) for one in larges]
        + [pl.BlockSpec(gain_part.shape, lambda at: (0, 0))],
        out_specs=[pl.BlockSpec((64, SLAB), lambda at: (0, at))] * 6
        + [
            pl.BlockSpec((128, SLAB), lambda at: (0, jnp.minimum(at, half - 1))),
            pl.BlockSpec((128, SLAB), lambda at: (0, jnp.maximum(at - half, 0))),
            pl.BlockSpec((64, 128), lambda at: (0, 0)),
        ],
        compiler_params=PARAMS,
    )(acts, *larges, gain_part)


def pack_kernel(acts, sums, other, out):
    out[:ROWS, :] = acts[...]
    high, low = two_parts(sums[...] + other[...])
    for side in range(2):
        rows = slice(32 * side, 32 * side + 32)
        out[ROWS:, 128 * side : 128 * side + 128] = high[rows]
        out[ROWS:, 256 + 128 * side : 384 + 128 * side] = low[rows]
    out[ROWS:, 512:] = jnp.zeros((32, 256), BF16)


def pack(acts, sums, other):
    return pl.pallas_call(
        pack_kernel,
        out_shape=shape(ROWS + 32, acts.shape[1]),
        in_specs=[VMEM] * 3,
        out_specs=VMEM,
        compiler_params=PARAMS,
    )(acts, sums, other)


def relay_kernel(opposite, left, right, packed, packed_far, out, rounded):
    half = D // 2
    rows = slice(64, 128)
    out[:, :half] = (opposite[:, :half].astype(F32) + left[rows, :].astype(F32)).astype(BF16)
    out[:, half:D] = (opposite[:, half:].astype(F32) + right[rows, :].astype(F32)).astype(BF16)
    for side in range(2):
        here = slice(128 * side, 128 * side + 128)
        beside = slice(256 + 128 * side, 384 + 128 * side)
        mine, theirs = (
            ref[ROWS:, here].astype(F32) + ref[ROWS:, beside].astype(F32)
            for ref in (packed, packed_far)
        )
        high, low = two_parts(mine + theirs)
        rows = slice(32 * side, 32 * side + 32)
        out[rows, D : D + 128] = high
        out[rows, D + 128 :] = low
        rounded[rows, :] = high.astype(F32) + low.astype(F32)


def relay(opposite, left, right, packed, packed_far):
    return pl.pallas_call(
        relay_kernel,
        out_shape=[shape(64, D + 256), shape(64, 128, dtype=F32)],
        in_specs=[VMEM] * 5,
        out_specs=[VMEM] * 2,
        compiler_params=PARAMS,
    )(opposite, left, right, packed, packed_far)


FAR_WIDE = D + 8 * 128
LAST_WIDE = D + 16 * 128


def spread_kernel(kept, left, right, got, sums, near, far, *outs):
    half = D // 2
    other = got[:, D : D + 128].astype(F32) + got[:, D + 128 :].astype(F32)
    high, low = two_parts((sums[...] + near[...]) + (other + far[...]))
    for at in range(4):
        rows = slice(16 * at, 16 * at + 16)
        first = kept[rows, :half].astype(F32) + left[rows, :].astype(F32)
        outs[at][:, :half] = (first + got[rows, :half].astype(F32)).astype(BF16)
        first = kept[rows, half:].astype(F32) + right[rows, :].astype(F32)
        outs[at][:, half:D] = (first + got[rows, half:D].astype(F32)).astype(BF16)
        for k in range(4):
            left_edge = D + 128 * k
            outs[at][:, left_edge : left_edge + 128] = high[16 * k : 16 * k + 16]
            outs[at][:, left_edge + 512 : left_edge + 640] = low[16 * k : 16 * k + 16]


def spread(*parts):
    return pl.pallas_call(
        spread_kernel,
        out_shape=[shape(16, FAR_WIDE)] * 4,
        in_specs=[VMEM] * 7,
        out_specs=[VMEM] * 4,
        compiler_params=PARAMS,
    )(*parts)


def split_sum_kernel(place, *refs):
    for at in range(4):
        rows = slice(16 * at, 16 * at + 16)
        spot = pl.ds(pl.multiple_of(place[19 + at], 16), 16)
        refs[4][spot, :] = total([ref[rows, :] for ref in refs[:4]]).astype(BF16)


def split_sum(place, parts):
    return pl.pallas_call(
        split_sum_kernel,
        out_shape=shape(64, D),
        in_specs=[SMEM] + [VMEM] * 4,
        out_specs=VMEM,
        compiler_params=PARAMS,
    )(place, *parts)


def ends_kernel(*refs):
    mixed_ref, back_refs, outs = refs[0], refs[1:5], refs[5:]
    mixed = total([mixed_ref[16 * at : 16 * at + 16, :] for at in range(4)])
    back = total([ref[:, :D] for ref in back_refs])
    for at in range(4):
        rows = slice(4 * at, 4 * at + 4)
        outs[at][:, :D] = jnp.concatenate([mixed[rows], back[rows]], 0).astype(BF16)
    for k in range(4):
        here = slice(D + 128 * k, D + 128 * k + 128)
        beside = slice(D + 512 + 128 * k, D + 640 + 128 * k)
        block = total([ref[:, here].astype(F32) + ref[:, beside].astype(F32) for ref in back_refs])
        for side in range(2):
            high, low = two_parts(block[8 * side : 8 * side + 8])
            edge = D + 128 * (2 * k + side)
            for out in outs:
                out[:, edge : edge + 128] = high
                out[:, edge + 1024 : edge + 1152] = low


def ends(mixed, back_parts):
    return pl.pallas_call(
        ends_kernel,
        out_shape=[shape(8, LAST_WIDE)] * 4,
        in_specs=[VMEM] * 5,
        out_specs=[VMEM] * 4,
        compiler_params=PARAMS,
    )(mixed, *back_parts)


def finish_kernel(first, second, third, fourth, tokens, cotangent, gain, out, d_out, ln_out, qk_out):
    parts = (first, second, third, fourth)
    rows = total([ref[:, :D] for ref in parts])
    x_float = tokens[...].astype(F32)
    scaled, inv_std = standardize(x_float)
    out[...] = (x_float + rows[:4]).astype(BF16)
    d_norm = norm_back(rows[4:], scaled, inv_std, gain[...])
    d_out[...] = (cotangent[...].astype(F32) + d_norm).astype(BF16)
    for k in range(8):
        here = slice(D + 128 * k, D + 128 * k + 128)
        beside = slice(D + 1024 + 128 * k, D + 1152 + 128 * k)
        block = total([ref[:, here].astype(F32) + ref[:, beside].astype(F32) for ref in parts])
        if k < 6:
            for row in range(8):
                edge = 128 * (8 * k + row)
                ln_out[:, edge : edge + 128] = block[row : row + 1]
        if k == 6:
            qk_out[...] = block[:2]


def finish(parts, tokens, cotangent, gain):
    return pl.pallas_call(
        finish_kernel,
        out_shape=[
            shape(4, D),
            shape(4, D),
            shape(1, D, dtype=F32),
            shape(2, HD, dtype=F32),
        ],
        in_specs=[VMEM] * 7,
        out_specs=[VMEM] * 4,
        compiler_params=PARAMS,
    )(*parts, tokens, cotangent, gain)


def add_kernel(keep, taken, *outs):
    row = 0
    for out in outs:
        rows = slice(row, row + out.shape[0])
        out[...] = (keep[rows, :].astype(F32) + taken[rows, :].astype(F32)).astype(BF16)
        row += out.shape[0]


def add(keep, taken, heights):
    width = QUARTER // 2
    return pl.pallas_call(
        add_kernel,
        grid=(2,),
        out_shape=[shape(height, QUARTER) for height in heights],
        in_specs=[pl.BlockSpec((keep.shape[0], width), lambda at: (0, at))] * 2,
        out_specs=[pl.BlockSpec((height, width), lambda at: (0, at)) for height in heights],
    )(keep, taken)


def grads_kernel(place, acts, acts_far, n_ref, c_ref, far, *refs):
    keep, give, n_all, c_all, kept, given, sems, out_sems = refs
    half = D // 2
    own = pl.ds(pl.multiple_of(place[0] * half, half), half)
    top = pl.ds(0, ROWS)
    moves = [(n_ref.at[:, own], n_all.at[top]), (c_ref.at[:, own], c_all.at[top])]
    for at in range(16):
        row = pl.multiple_of(place[3 + at], 32)
        spot = pl.ds(ROWS + 16 * at, 16)
        moves.append((far.at[pl.ds(row, 16)], n_all.at[spot]))
        moves.append((far.at[pl.ds(row + 16, 16)], c_all.at[spot]))
    loads = []
    for at, (source, target) in enumerate(moves):
        copy = pltpu.make_async_copy(source, target, sems.at[at])
        copy.start()
        loads.append(copy)
    whole = jnp.concatenate([acts[:ROWS, :], acts_far[:ROWS, :]], 0)
    ins, heads = 3 * HD // 2, 2 * HD
    units = (whole.shape[1] - heads) // 2
    for copy in loads:
        copy.wait()
    stores = []
    for at, (buffer, target, column) in enumerate(
        ((given, give, 1 - place[1]), (kept, keep, place[1]))
    ):
        span = pl.ds(pl.multiple_of(column * QUARTER, QUARTER), QUARTER)
        row = 0
        for left, right in (
            (whole[:, :ins], n_all),
            (whole[:, heads : heads + units], n_all),
            (whole[:, ins:heads], c_all),
            (whole[:, heads + units :], c_all),
        ):
            height = left.shape[1]
            buffer[row : row + height, :] = row_contract(left, right[:, span]).astype(BF16)
            row += height
        copy = pltpu.make_async_copy(buffer, target, out_sems.at[at])
        copy.start()
        stores.append(copy)
    for copy in stores:
        copy.wait()


def grads(place, acts, acts_far, n_all, c_all, far):
    height = acts.shape[1]
    return pl.pallas_call(
        grads_kernel,
        out_shape=[shape(height, QUARTER)] * 2,
        in_specs=[SMEM] + [VMEM] * 2 + [ANY] * 3,
        out_specs=[ANY] * 2,
        scratch_shapes=[
            pltpu.VMEM((2 * ROWS, D // 2), BF16),
            pltpu.VMEM((2 * ROWS, D // 2), BF16),
            pltpu.VMEM((height, QUARTER), BF16),
            pltpu.VMEM((height, QUARTER), BF16),
            pltpu.SemaphoreType.DMA((34,)),
            pltpu.SemaphoreType.DMA((2,)),
        ],
        compiler_params=PARAMS,
    )(place, acts, acts_far, n_all, c_all, far)


def all_to_all(block, unit):
    groups = [
        [first + unit * at for at in range(4)]
        for first in range(64)
        if first // unit % 4 == 0
    ]
    return lax.all_to_all(block, "mp", 0, 0, axis_index_groups=groups, tiled=True)


def all_planes(block):
    planes = [[Y * up + Z * deep + X * at for up in range(4) for at in range(4)] for deep in range(4)]
    return lax.all_gather(block, "mp", axis=0, tiled=True, axis_index_groups=planes)


def local(tokens, cotangent, ln_gain, qk_gain, w_qkv, w_mlp_in, w_attn_out, w_mlp_out):
    tie = lax.optimization_barrier
    dp, mp = lax.axis_index("dp"), lax.axis_index("mp")
    up, at = mp // Y, mp % 4
    starts = [32 * (4 * (up ^ high) + (at ^ low)) for high in range(4) for low in range(4)]
    starts += [16 * (at ^ step) for step in range(4)] + [16 * (up ^ step) for step in range(4)]
    place = jnp.stack([dp // 2, dp % 2, mp % 2] + starts).astype(jnp.int32)
    cols, units = w_qkv.shape[1], w_mlp_in.shape[0]
    offset = mp % 2 * cols
    gains = jnp.concatenate(
        [
            lax.dynamic_slice_in_dim(qk_gain, offset, cols, 1),
            lax.dynamic_slice_in_dim(qk_gain, cols - offset, cols, 1),
        ],
        1,
    )
    gain_row = ln_gain.reshape(1, D)
    w_flat = w_qkv.reshape(3 * cols, D)

    n_rows, c_rows, away = apart(place, tie(pieces(start(tokens, cotangent, gain_row), Z)))
    n_parts, c_rows = tie((pieces(n_rows, X), all_to_all(c_rows, Y)))
    n_rows = join(n_parts)
    n_rows, c_rows, away = tie((n_rows, c_rows, away))
    n_parts, c_parts, there = tie((pieces(n_rows, Y), two_steps(c_rows), swapped(away, "dp", 2)))
    n_all, c_all, qk_own, vd_own = first(place, n_parts, c_parts, w_flat, w_attn_out)

    qk_peer, vd_peer = swapped(qk_own, "mp", X), swapped(vd_own, "mp", X)
    there, n_next = tie((there, n_all))
    far = all_planes(there)
    ad = hidden(n_next, c_all, w_mlp_in, w_mlp_out)
    qk_peer, vd_peer, ad = tie((qk_peer, vd_peer, ad))
    acts, gain_part = head(place, qk_own, qk_peer, vd_own, vd_peer, gains, ad)
    outs = back(acts, w_attn_out, w_mlp_out, w_flat, w_mlp_in, n_all, gain_row, gain_part)
    kept, opposite, left, right, sums = outs[4:]
    left, right = swapped(left, "mp", X), swapped(right, "mp", 3 * X)
    near, late = swapped(outs[1], "mp", Y), swapped(outs[3], "mp", 3 * Y)
    packed = pack(acts, sums, swapped(sums, "dp", 1))
    packed_far = swapped(packed, "dp", 2)
    left, right, near, late, packed_far = tie((left, right, near, late, packed_far))
    relayed, sums = relay(opposite, left, right, packed, packed_far)
    relayed, middle, packed_far = tie((relayed, outs[2], packed_far))
    got, middle = swapped(relayed, "mp", 2 * X), swapped(middle, "mp", 2 * Y)
    other_sums = swapped(sums, "mp", X), swapped(sums, "mp", 3 * X)
    keep, give = grads(place, packed, packed_far, n_all, c_all, far)
    got, middle, other_sums, keep, give = tie((got, middle, other_sums, keep, give))
    taken = swapped(give, "dp", 1)
    spreads = spread(kept, left, right, got, sums, *other_sums)
    spreads, middle = tie((spreads, middle))
    back_parts = exchanged(spreads, Y)
    mixed = all_to_all(split_sum(place, [outs[0], near, middle, late]), X)
    last = exchanged(ends(mixed, back_parts), Z)
    parts = add(keep, taken, (3 * cols, units, cols, units))
    last, parts = tie((last, parts))
    output, d_tokens, g_ln, g_qk = finish(last, tokens, cotangent, gain_row)
    return (
        output,
        d_tokens,
        g_ln.reshape(D),
        g_qk,
        parts[0].reshape(3, cols, QUARTER),
        *parts[1:],
    )


def solution(mesh):
    return jax.shard_map(
        local,
        mesh=mesh,
        in_specs=(
            P(("dp", "mp"), None),
            P(("dp", "mp"), None),
            P(),
            P(),
            P(None, "mp", None),
            P("mp", None),
            P("mp", None),
            P("mp", None),
        ),
        out_specs=(
            P(("dp", "mp"), None),
            P(("dp", "mp"), None),
            P(),
            P(),
            P(None, "mp", "dp"),
            P("mp", "dp"),
            P("mp", "dp"),
            P("mp", "dp"),
        ),
        check_vma=False,
    )
```

profile of v0, /device:TPU:1, one launch (start us, length us, event | category | flops | bytes accessed | tf_op | source)
XLA Modules:
  0.0 216.4 jit_solution(6805671274080107009)
XLA Ops:
  9.8 5.3 %collective-permute-start.2 = (bf16[8,6144]{1,0:T(8,128)(2,1)S(1)}, bf16[8,6144]{1,0:T(8,128)(2,1)S(1)}, u32[]{:S(2)}, u32[]{:S(2)}) collective-permute-start(bf16[8,6144]{1,0:T(8,128)(2,1)S(1)} %shard_map.143.refs_0_), channel_id=1, source_target_pairs={{0,12},{1,13},{2,14},{3,15},{4,8},{5,9},{6,10},{7,11},{8,4},{9,5},... | collective-permute-start | bytes 294920 | tf_op jit(solution)/shard_map/ppermute | solution.py:31
  17.2 5.6 %collective-permute-done.1.refs_2_ = bf16[8,6144]{1,0:T(8,128)(2,1)S(1)} collective-permute-done((bf16[8,6144]{1,0:T(8,128)(2,1)S(1)}, bf16[8,6144]{1,0:T(8,128)(2,1)S(1)}, u32[]{:S(2)}, u32[]{:S(2)}) %collective-permute-start.1) | collective-permute-done | bytes 98336 | tf_op jit(solution)/shard_map/ppermute | solution.py:31
  24.5 4.2 %all-to-all-start = ((bf16[4,16,6144]{2,1,0:T(8,128)(2,1)}), bf16[4,16,6144]{2,1,0:T(8,128)(2,1)S(1)}, u32[]{:S(2)}, u32[]{:S(2)}) async-start(bf16[4,16,6144]{2,1,0:T(8,128)(2,1)} %bitcast.28), calls=%async_computation | async-start | bytes 1572864 | tf_op jit(solution)/shard_map/all_to_all | solution.py:639
  31.9 7.4 %collective-permute-done.5.refs_3_ = bf16[16,6144]{1,0:T(8,128)(2,1)S(1)} collective-permute-done((bf16[16,6144]{1,0:T(8,128)(2,1)S(1)}, bf16[16,6144]{1,0:T(8,128)(2,1)S(1)}, u32[]{:S(2)}, u32[]{:S(2)}) %collective-permute-start.5) | collective-permute-done | bytes 196640 | tf_op jit(solution)/shard_map/ppermute | solution.py:31
  39.7 2.8 %collective-permute-start.9 = (bf16[64,6144]{1,0:T(8,128)(2,1)S(1)}, bf16[64,6144]{1,0:T(8,128)(2,1)S(1)}, u32[]{:S(2)}, u32[]{:S(2)}) collective-permute-start(bf16[64,6144]{1,0:T(8,128)(2,1)S(1)} %bitcast.35), channel_id=1, source_target_pairs={{0,2},{1,3},{2,0},{3,1},{4,6},{5,7},{6,4},{7,5},{8,10},{9,11},{10,... | collective-permute-start | bytes 2359304 | tf_op jit(solution)/shard_map/ppermute | solution.py:31
  45.8 5.6 %collective-permute-start.12 = (bf16[32,3072]{1,0:T(8,128)(2,1)S(1)}, bf16[32,3072]{1,0:T(8,128)(2,1)}, u32[]{:S(2)}, u32[]{:S(2)}) collective-permute-start(bf16[32,3072]{1,0:T(8,128)(2,1)S(1)} %get-tuple-element.113), channel_id=1, source_target_pairs={{0,128},{64,192},{128,0},{192,64},{1,129},{65,193},{129,1},{193,65... | collective-permute-start | bytes 589832 | tf_op jit(solution)/shard_map/ppermute | solution.py:31
  51.5 6.7 %collective-permute-done.9.refs_6_ = bf16[64,6144]{1,0:T(8,128)(2,1)S(1)} collective-permute-done((bf16[64,6144]{1,0:T(8,128)(2,1)S(1)}, bf16[64,6144]{1,0:T(8,128)(2,1)S(1)}, u32[]{:S(2)}, u32[]{:S(2)}) %collective-permute-start.9) | collective-permute-done | bytes 786464 | tf_op jit(solution)/shard_map/ppermute | solution.py:31
  59.5 3.8 %collective-permute-start.11 = (bf16[128,3072]{1,0:T(8,128)(2,1)}, bf16[128,3072]{1,0:T(8,128)(2,1)}, u32[]{:S(2)}, u32[]{:S(2)}) collective-permute-start(bf16[128,3072]{1,0:T(8,128)(2,1)} %get-tuple-element.190), channel_id=1, source_target_pairs={{0,3},{1,2},{2,1},{3,0},{4,7},{5,6},{6,5},{7,4},{8,11},{9,10},{10,... | collective-permute-start | bytes 2359304 | tf_op jit(solution)/shard_map/ppermute | solution.py:31
  63.3 15.0 %collective-permute-done.8.refs_4_ = bf16[64,6144]{1,0:T(8,128)(2,1)S(1)} collective-permute-done((bf16[64,6144]{1,0:T(8,128)(2,1)S(1)}, bf16[64,6144]{1,0:T(8,128)(2,1)S(1)}, u32[]{:S(2)}, u32[]{:S(2)}) %collective-permute-start.8) | collective-permute-done | bytes 786464 | tf_op jit(solution)/shard_map/ppermute | solution.py:31
  79.9 7.3 %shard_map.146 = (bf16[256,6144]{1,0:T(8,128)(2,1)}, bf16[256,6144]{1,0:T(8,128)(2,1)}, f32[256,128]{1,0:T(8,128)S(1)}, bf16[256,128]{1,0:T(8,128)(2,1)S(1)}) custom-call(s32[27]{0:T(128)S(1)} %stack.111.place.refs_0_, bf16[64,6144]{1,0:T(8,128)(2,1)S(1)} %shard_map.145.refs_1_, bf16[64,6144]{1,0:T(8,128)(2,1)} %collective-permute-done.6.refs_2_, ...), custom_call_target="tpu_custom_call" | custom-call | tf_op jit(solution)/shard_map/pallas_call | solution.py:209
  91.0 4.7 %shard_map.147.ad = bf16[256,512]{1,0:T(8,128)(2,1)S(1)} custom-call(bf16[256,6144]{1,0:T(8,128)(2,1)S(1)} %copy-done, bf16[256,6144]{1,0:T(8,128)(2,1)} %get-tuple-element.127.c_ref, bf16[256,6144]{1,0:T(8,128)(2,1)} %w_mi.1, bf16[256,6144]{1,0:T(8,128)(2,1)} %w_mo.1), custom_call_target="tpu_custom_call" | custom-call | tf_op jit(solution)/shard_map/pallas_call | solution.py:259
  98.1 9.8 %shard_map.149 = (bf16[64,6144]{1,0:T(8,128)(2,1)S(1)}, bf16[64,6144]{1,0:T(8,128)(2,1)S(1)}, bf16[64,6144]{1,0:T(8,128)(2,1)}, bf16[64,6144]{1,0:T(8,128)(2,1)S...) custom-call(bf16[256,768]{1,0:T(8,128)(2,1)S(1)} %get-tuple-element., ...), custom_call_target="tpu_custom_call" | custom-call | tf_op jit(solution)/shard_map/pallas_call | solution.py:373
  113.2 5.0 %collective-permute-start.19 = (f32[64,128]{1,0:T(8,128)S(1)}, f32[64,128]{1,0:T(8,128)S(1)}, u32[]{:S(2)}, u32[]{:S(2)}) collective-permute-start(f32[64,128]{1,0:T(8,128)S(1)} %get-tuple-element.138.sums), channel_id=1, source_target_pairs={{0,64},{64,0},{128,192},{192,128},{1,65},{65,1},{129,193},{193,129... | collective-permute-start | bytes 98312 | tf_op jit(solution)/shard_map/ppermute | solution.py:31
  119.2 5.8 %collective-permute-start.20 = (bf16[288,768]{1,0:T(8,128)(2,1)S(1)}, bf16[288,768]{1,0:T(8,128)(2,1)S(1)}, u32[]{:S(2)}, u32[]{:S(2)}) collective-permute-start(bf16[288,768]{1,0:T(8,128)(2,1)S(1)} %shard_map.150.packed.acts), channel_id=1, source_target_pairs={{0,128},{64,192},{128,0},{192,64},{1,129},{65,193},{129,1},{193,65... | collective-permute-start | bytes 1327112 | tf_op jit(solution)/shard_map/ppermute | solution.py:31
  125.0 19.4 %collective-permute-done.20.packed_far.acts_far = bf16[288,768]{1,0:T(8,128)(2,1)S(1)} collective-permute-done((bf16[288,768]{1,0:T(8,128)(2,1)S(1)}, bf16[288,768]{1,0:T(8,128)(2,1)S(1)}, u32[]{:S(2)}, u32[]{:S(2)}) %collective-permute-start.20) | collective-permute-done | bytes 442400 | tf_op jit(solution)/shard_map/ppermute | solution.py:31
  145.8 2.7 %collective-permute-start.21 = (bf16[64,6400]{1,0:T(8,128)(2,1)}, bf16[64,6400]{1,0:T(8,128)(2,1)S(1)}, u32[]{:S(2)}, u32[]{:S(2)}) collective-permute-start(bf16[64,6400]{1,0:T(8,128)(2,1)} %get-tuple-element.147), channel_id=1, source_target_pairs={{0,2},{1,3},{2,0},{3,1},{4,6},{5,7},{6,4},{7,5},{8,10},{9,11},{10,... | collective-permute-start | bytes 2457608 | tf_op jit(solution)/shard_map/ppermute | solution.py:31
  149.5 6.9 %shard_map.152 = (bf16[768,1536]{1,0:T(8,128)(2,1)S(1)}, bf16[768,1536]{1,0:T(8,128)(2,1)}) custom-call(s32[27]{0:T(128)S(1)} %stack.111.place.refs_0_, bf16[288,768]{1,0:T(8,128)(2,1)S(1)} %shard_map.150.packed.acts, bf16[288,768]{1,0:T(8,128)(2,1)S(1)} %collective-permute-done.20.packed_far.acts_far, bf16[256,6144]{1,0:T(8,128)(2,1)} %get-tuple-element.126.n_ref, ...), custom_call_target="tpu_custom_call" | custom-call | tf_op jit(solution)/shard_map/pallas_call | solution.py:616
  157.8 10.7 %collective-permute-done.24.far = f32[64,128]{1,0:T(8,128)S(1)} collective-permute-done((f32[64,128]{1,0:T(8,128)S(1)}, f32[64,128]{1,0:T(8,128)S(1)}, u32[]{:S(2)}, u32[]{:S(2)}) %collective-permute-start.24) | collective-permute-done | bytes 32800 | tf_op jit(solution)/shard_map/ppermute | solution.py:31
  174.5 3.5 %all-to-all-start.1 = ((bf16[4,16,6144]{2,1,0:T(8,128)(2,1)}), bf16[4,16,6144]{2,1,0:T(8,128)(2,1)S(1)}, u32[]{:S(2)}, u32[]{:S(2)}) async-start(bf16[4,16,6144]{2,1,0:T(8,128)(2,1)} %bitcast.31), calls=%async_computation.1 | async-start | bytes 1572864 | tf_op jit(solution)/shard_map/all_to_all | solution.py:639
  182.0 3.4 %collective-permute-done.25.refs_2_ = bf16[16,7168]{1,0:T(8,128)(2,1)S(1)} collective-permute-done((bf16[16,7168]{1,0:T(8,128)(2,1)S(1)}, bf16[16,7168]{1,0:T(8,128)(2,1)S(1)}, u32[]{:S(2)}, u32[]{:S(2)}) %collective-permute-start.25) | collective-permute-done | bytes 229408 | tf_op jit(solution)/shard_map/ppermute | solution.py:31
  185.3 5.6 %collective-permute-done.26.refs_3_ = bf16[16,7168]{1,0:T(8,128)(2,1)S(1)} collective-permute-done((bf16[16,7168]{1,0:T(8,128)(2,1)S(1)}, bf16[16,7168]{1,0:T(8,128)(2,1)S(1)}, u32[]{:S(2)}, u32[]{:S(2)}) %collective-permute-start.26) | collective-permute-done | bytes 229408 | tf_op jit(solution)/shard_map/ppermute | solution.py:31
  193.4 3.3 %collective-permute-start.28 = (bf16[8,8192]{1,0:T(8,128)(2,1)S(1)}, bf16[8,8192]{1,0:T(8,128)(2,1)S(1)}, u32[]{:S(2)}, u32[]{:S(2)}) collective-permute-start(bf16[8,8192]{1,0:T(8,128)(2,1)S(1)} %get-tuple-element.169), channel_id=1, source_target_pairs={{0,4},{1,5},{2,6},{3,7},{4,0},{5,1},{6,2},{7,3},{8,12},{9,13},{10,... | collective-permute-start | bytes 393224 | tf_op jit(solution)/shard_map/ppermute | solution.py:31
  198.8 3.6 %shard_map.156 = (bf16[192,1536]{1,0:T(8,128)(2,1)}, bf16[256,1536]{1,0:T(8,128)(2,1)}, bf16[64,1536]{1,0:T(8,128)(2,1)}, bf16[256,1536]{1,0:T(8,128)(2,1)}) custom-call(bf16[768,1536]{1,0:T(8,128)(2,1)} %copy-done.1, bf16[768,1536]{1,0:T(8,128)(2,1)} %collective-permute-done.31.taken), custom_call_target="tpu_custom_call" | custom-call | tf_op jit(solution)/shard_map/pallas_call | solution.py:562
  202.4 6.0 %collective-permute-done.29.third = bf16[8,8192]{1,0:T(8,128)(2,1)S(1)} collective-permute-done((bf16[8,8192]{1,0:T(8,128)(2,1)S(1)}, bf16[8,8192]{1,0:T(8,128)(2,1)S(1)}, u32[]{:S(2)}, u32[]{:S(2)}) %collective-permute-start.29) | collective-permute-done | bytes 131104 | tf_op jit(solution)/shard_map/ppermute | solution.py:31
  (112 shorter events, 48.2 us)
Async XLA Ops:
  24.5 15.2 %all-to-all-start = ((bf16[4,16,6144]{2,1,0:T(8,128)(2,1)}), bf16[4,16,6144]{2,1,0:T(8,128)(2,1)S(1)}, u32[]{:S(2)}, u32[]{:S(2)}) async-start(bf16[4,16,6144]{2,1,0:T(8,128)(2,1)} %bitcast.28), calls=%async_computation | async-start | bytes 1572864 | tf_op jit(solution)/shard_map/all_to_all | solution.py:639
  28.6 120.8 %all-gather.2.cloned.1.call-start = ((), (), s32[]{:S(2)}) async-start(), calls=%async_computation.2 | async-start | bytes 3342336 | tf_op jit(solution)/shard_map/all_gather | solution.py:644
  39.7 18.4 %collective-permute-start.9 = (bf16[64,6144]{1,0:T(8,128)(2,1)S(1)}, bf16[64,6144]{1,0:T(8,128)(2,1)S(1)}, u32[]{:S(2)}, u32[]{:S(2)}) collective-permute-start(bf16[64,6144]{1,0:T(8,128)(2,1)S(1)} %bitcast.35), channel_id=1, source_target_pairs={{0,2},{1,3},{2,0},{3,1},{4,6},{5,7},{6,4},{7,5},{8,10},{9,11},{10,... | collective-permute-start | bytes 2359304 | tf_op jit(solution)/shard_map/ppermute | solution.py:31
  42.6 35.7 %collective-permute-start.8 = (bf16[64,6144]{1,0:T(8,128)(2,1)S(1)}, bf16[64,6144]{1,0:T(8,128)(2,1)S(1)}, u32[]{:S(2)}, u32[]{:S(2)}) collective-permute-start(bf16[64,6144]{1,0:T(8,128)(2,1)S(1)} %shard_map.145.refs_1_), channel_id=1, source_target_pairs={{0,48},{1,49},{2,50},{3,51},{4,52},{5,53},{6,54},{7,55},{8,56},{9,... | collective-permute-start | bytes 2359304 | tf_op jit(solution)/shard_map/ppermute | solution.py:31
  44.9 33.4 %collective-permute-start.7 = (bf16[64,6144]{1,0:T(8,128)(2,1)S(1)}, bf16[64,6144]{1,0:T(8,128)(2,1)}, u32[]{:S(2)}, u32[]{:S(2)}) collective-permute-start(bf16[64,6144]{1,0:T(8,128)(2,1)S(1)} %shard_map.145.refs_1_), channel_id=1, source_target_pairs={{0,32},{1,33},{2,34},{3,35},{4,36},{5,37},{6,38},{7,39},{8,40},{9,... | collective-permute-start | bytes 2359304 | tf_op jit(solution)/shard_map/ppermute | solution.py:31
  45.4 32.8 %collective-permute-start.6 = (bf16[64,6144]{1,0:T(8,128)(2,1)S(1)}, bf16[64,6144]{1,0:T(8,128)(2,1)}, u32[]{:S(2)}, u32[]{:S(2)}) collective-permute-start(bf16[64,6144]{1,0:T(8,128)(2,1)S(1)} %shard_map.145.refs_1_), channel_id=1, source_target_pairs={{0,16},{1,17},{2,18},{3,19},{4,20},{5,21},{6,22},{7,23},{8,24},{9,... | collective-permute-start | bytes 2359304 | tf_op jit(solution)/shard_map/ppermute | solution.py:31
  45.8 17.4 %collective-permute-start.12 = (bf16[32,3072]{1,0:T(8,128)(2,1)S(1)}, bf16[32,3072]{1,0:T(8,128)(2,1)}, u32[]{:S(2)}, u32[]{:S(2)}) collective-permute-start(bf16[32,3072]{1,0:T(8,128)(2,1)S(1)} %get-tuple-element.113), channel_id=1, source_target_pairs={{0,128},{64,192},{128,0},{192,64},{1,129},{65,193},{129,1},{193,65... | collective-permute-start | bytes 589832 | tf_op jit(solution)/shard_map/ppermute | solution.py:31
  59.5 19.5 %collective-permute-start.11 = (bf16[128,3072]{1,0:T(8,128)(2,1)}, bf16[128,3072]{1,0:T(8,128)(2,1)}, u32[]{:S(2)}, u32[]{:S(2)}) collective-permute-start(bf16[128,3072]{1,0:T(8,128)(2,1)} %get-tuple-element.190), channel_id=1, source_target_pairs={{0,3},{1,2},{2,1},{3,0},{4,7},{5,6},{6,5},{7,4},{8,11},{9,10},{10,... | collective-permute-start | bytes 2359304 | tf_op jit(solution)/shard_map/ppermute | solution.py:31
  63.3 16.6 %collective-permute-start.10 = (bf16[128,3072]{1,0:T(8,128)(2,1)}, bf16[128,3072]{1,0:T(8,128)(2,1)S(1)}, u32[]{:S(2)}, u32[]{:S(2)}) collective-permute-start(bf16[128,3072]{1,0:T(8,128)(2,1)} %get-tuple-element.191), channel_id=1, source_target_pairs={{0,1},{1,0},{2,3},{3,2},{4,5},{5,4},{6,7},{7,6},{8,9},{9,8},{10,11... | collective-permute-start | bytes 2359304 | tf_op jit(solution)/shard_map/ppermute | solution.py:31
  108.8 35.5 %collective-permute-start.15 = (bf16[128,3072]{1,0:T(8,128)(2,1)S(1)}, bf16[128,3072]{1,0:T(8,128)(2,1)S(1)}, u32[]{:S(2)}, u32[]{:S(2)}) collective-permute-start(bf16[128,3072]{1,0:T(8,128)(2,1)S(1)} %get-tuple-element.134), channel_id=1, source_target_pairs={{0,1},{1,0},{2,3},{3,2},{4,5},{5,4},{6,7},{7,6},{8,9},{9,8},{10,11... | collective-permute-start | bytes 2359304 | tf_op jit(solution)/shard_map/ppermute | solution.py:31
  109.1 35.2 %collective-permute-start.16 = (bf16[128,3072]{1,0:T(8,128)(2,1)}, bf16[128,3072]{1,0:T(8,128)(2,1)S(1)}, u32[]{:S(2)}, u32[]{:S(2)}) collective-permute-start(bf16[128,3072]{1,0:T(8,128)(2,1)} %get-tuple-element.135), channel_id=1, source_target_pairs={{0,3},{1,2},{2,1},{3,0},{4,7},{5,6},{6,5},{7,4},{8,11},{9,10},{10,... | collective-permute-start | bytes 2359304 | tf_op jit(solution)/shard_map/ppermute | solution.py:31
  110.4 34.0 %collective-permute-start.17 = (bf16[64,6144]{1,0:T(8,128)(2,1)S(1)}, bf16[64,6144]{1,0:T(8,128)(2,1)S(1)}, u32[]{:S(2)}, u32[]{:S(2)}) collective-permute-start(bf16[64,6144]{1,0:T(8,128)(2,1)S(1)} %get-tuple-element.136), channel_id=1, source_target_pairs={{0,16},{1,17},{2,18},{3,19},{4,20},{5,21},{6,22},{7,23},{8,24},{9,... | collective-permute-start | bytes 2359304 | tf_op jit(solution)/shard_map/ppermute | solution.py:31
  111.5 32.9 %collective-permute-start.18 = (bf16[64,6144]{1,0:T(8,128)(2,1)S(1)}, bf16[64,6144]{1,0:T(8,128)(2,1)S(1)}, u32[]{:S(2)}, u32[]{:S(2)}) collective-permute-start(bf16[64,6144]{1,0:T(8,128)(2,1)S(1)} %get-tuple-element.137), channel_id=1, source_target_pairs={{0,48},{1,49},{2,50},{3,51},{4,52},{5,53},{6,54},{7,55},{8,56},{9,... | collective-permute-start | bytes 2359304 | tf_op jit(solution)/shard_map/ppermute | solution.py:31
  119.2 25.2 %collective-permute-start.20 = (bf16[288,768]{1,0:T(8,128)(2,1)S(1)}, bf16[288,768]{1,0:T(8,128)(2,1)S(1)}, u32[]{:S(2)}, u32[]{:S(2)}) collective-permute-start(bf16[288,768]{1,0:T(8,128)(2,1)S(1)} %shard_map.150.packed.acts), channel_id=1, source_target_pairs={{0,128},{64,192},{128,0},{192,64},{1,129},{65,193},{129,1},{193,65... | collective-permute-start | bytes 1327112 | tf_op jit(solution)/shard_map/ppermute | solution.py:31
  145.8 22.7 %collective-permute-start.21 = (bf16[64,6400]{1,0:T(8,128)(2,1)}, bf16[64,6400]{1,0:T(8,128)(2,1)S(1)}, u32[]{:S(2)}, u32[]{:S(2)}) collective-permute-start(bf16[64,6400]{1,0:T(8,128)(2,1)} %get-tuple-element.147), channel_id=1, source_target_pairs={{0,2},{1,3},{2,0},{3,1},{4,6},{5,7},{6,4},{7,5},{8,10},{9,11},{10,... | collective-permute-start | bytes 2457608 | tf_op jit(solution)/shard_map/ppermute | solution.py:31
  148.5 20.0 %collective-permute-start.22 = (bf16[64,6144]{1,0:T(8,128)(2,1)}, bf16[64,6144]{1,0:T(8,128)(2,1)}, u32[]{:S(2)}, u32[]{:S(2)}) collective-permute-start(bf16[64,6144]{1,0:T(8,128)(2,1)} %get-tuple-element.148), channel_id=1, source_target_pairs={{0,32},{1,33},{2,34},{3,35},{4,36},{5,37},{6,38},{7,39},{8,40},{9,... | collective-permute-start | bytes 2359304 | tf_op jit(solution)/shard_map/ppermute | solution.py:31
  148.5 19.9 %collective-permute-start.24 = (f32[64,128]{1,0:T(8,128)S(1)}, f32[64,128]{1,0:T(8,128)S(1)}, u32[]{:S(2)}, u32[]{:S(2)}) collective-permute-start(f32[64,128]{1,0:T(8,128)S(1)} %get-tuple-element.149.sums), channel_id=1, source_target_pairs={{0,3},{1,2},{2,1},{3,0},{4,7},{5,6},{6,5},{7,4},{8,11},{9,10},{10,... | collective-permute-start | bytes 98312 | tf_op jit(solution)/shard_map/ppermute | solution.py:31
  149.5 19.0 %collective-permute-start.23 = (f32[64,128]{1,0:T(8,128)S(1)}, f32[64,128]{1,0:T(8,128)S(1)}, u32[]{:S(2)}, u32[]{:S(2)}) collective-permute-start(f32[64,128]{1,0:T(8,128)S(1)} %get-tuple-element.149.sums), channel_id=1, source_target_pairs={{0,1},{1,0},{2,3},{3,2},{4,5},{5,4},{6,7},{7,6},{8,9},{9,8},{10,11... | collective-permute-start | bytes 98312 | tf_op jit(solution)/shard_map/ppermute | solution.py:31
  168.5 30.3 %collective-permute-start.31 = (bf16[768,1536]{1,0:T(8,128)(2,1)}, bf16[768,1536]{1,0:T(8,128)(2,1)}, u32[]{:S(2)}, u32[]{:S(2)}) collective-permute-start(bf16[768,1536]{1,0:T(8,128)(2,1)} %get-tuple-element.173), channel_id=1, source_target_pairs={{0,64},{64,0},{128,192},{192,128},{1,65},{65,1},{129,193},{193,129... | collective-permute-start | bytes 7077896 | tf_op jit(solution)/shard_map/ppermute | solution.py:31
  174.5 18.6 %all-to-all-start.1 = ((bf16[4,16,6144]{2,1,0:T(8,128)(2,1)}), bf16[4,16,6144]{2,1,0:T(8,128)(2,1)S(1)}, u32[]{:S(2)}, u32[]{:S(2)}) async-start(bf16[4,16,6144]{2,1,0:T(8,128)(2,1)} %bitcast.31), calls=%async_computation.1 | async-start | bytes 1572864 | tf_op jit(solution)/shard_map/all_to_all | solution.py:639
  178.1 12.7 %collective-permute-start.26 = (bf16[16,7168]{1,0:T(8,128)(2,1)S(1)}, bf16[16,7168]{1,0:T(8,128)(2,1)S(1)}, u32[]{:S(2)}, u32[]{:S(2)}) collective-permute-start(bf16[16,7168]{1,0:T(8,128)(2,1)S(1)} %copy-done.18), channel_id=1, source_target_pairs={{0,32},{1,33},{2,34},{3,35},{4,36},{5,37},{6,38},{7,39},{8,40},{9,... | collective-permute-start | bytes 688136 | tf_op jit(solution)/shard_map/ppermute | solution.py:31
  180.2 12.9 %collective-permute-start.27 = (bf16[16,7168]{1,0:T(8,128)(2,1)}, bf16[16,7168]{1,0:T(8,128)(2,1)S(1)}, u32[]{:S(2)}, u32[]{:S(2)}) collective-permute-start(bf16[16,7168]{1,0:T(8,128)(2,1)} %copy-done.16), channel_id=1, source_target_pairs={{0,48},{1,49},{2,50},{3,51},{4,52},{5,53},{6,54},{7,55},{8,56},{9,... | collective-permute-start | bytes 688136 | tf_op jit(solution)/shard_map/ppermute | solution.py:31
  196.7 11.8 %collective-permute-start.29 = (bf16[8,8192]{1,0:T(8,128)(2,1)S(1)}, bf16[8,8192]{1,0:T(8,128)(2,1)S(1)}, u32[]{:S(2)}, u32[]{:S(2)}) collective-permute-start(bf16[8,8192]{1,0:T(8,128)(2,1)S(1)} %get-tuple-element.170), channel_id=1, source_target_pairs={{0,8},{1,9},{2,10},{3,11},{4,12},{5,13},{6,14},{7,15},{8,0},{9,1},... | collective-permute-start | bytes 393224 | tf_op jit(solution)/shard_map/ppermute | solution.py:31
  196.7 11.7 %collective-permute-start.30 = (bf16[8,8192]{1,0:T(8,128)(2,1)S(1)}, bf16[8,8192]{1,0:T(8,128)(2,1)S(1)}, u32[]{:S(2)}, u32[]{:S(2)}) collective-permute-start(bf16[8,8192]{1,0:T(8,128)(2,1)S(1)} %get-tuple-element.171), channel_id=1, source_target_pairs={{0,12},{1,13},{2,14},{3,15},{4,8},{5,9},{6,10},{7,11},{8,4},{9,5},... | collective-permute-start | bytes 393224 | tf_op jit(solution)/shard_map/ppermute | solution.py:31
  (33 other events, 251.0 us)
Sparse Core Ops, SparseCore 0:
  87.3 58.3 all-gather.1
where the time goes:
time: 218 us; the launch traced here: 216 us
  waiting for transfers between devices  86.5 us (40%)
  starting transfers between devices  63.8 us (29%)
  Pallas kernels  42.2 us (19%)
  between operations  14.3 us (7%)
  local copies, waits for them, and re-layouts  9.5 us (4%)
    ppermute x32, waiting for transfers between devices, swapped(): lax.ppermute(block, axis, [(low, low ^ mask) for low in range(count)])  86.3 us
    ppermute x32, starting transfers between devices, swapped(): lax.ppermute(block, axis, [(low, low ^ mask) for low in range(count)])  56.2 us
    pallas_call x1, Pallas kernels, back(): pl.pallas_call(back_kernel, grid=(STEPS,), out_shape=[shape(64, D)] * 6 +...  9.84 us
    unnamed x45, local copies, waits for them, and re-layouts  8.03 us
    all_to_all x2, starting transfers between devices, all_to_all(): lax.all_to_all(block, 'mp', 0, 0, axis_index_groups=groups, tiled=True)  7.68 us
    pallas_call x1, Pallas kernels, first(): pl.pallas_call(first_kernel, out_shape=[shape(ROWS, D), shape(ROWS, D), s...  7.32 us
    pallas_call x1, Pallas kernels, grads(): pl.pallas_call(grads_kernel, out_shape=[shape(height, QUARTER)] * 2, in_s...  6.88 us
    pallas_call x1, Pallas kernels, hidden(): pl.pallas_call(hidden_kernel, out_shape=shape(ROWS, 2 * units), in_specs=...  4.67 us
  transfers between devices with their start and end apart: 35, of which 16 were waited for; matrix products, arithmetic and copies ran while one was open for 1% of the time, Pallas kernels for 15%

commit v1 on v0

--- a/solution.py
+++ b/solution.py
@@ -98,9 +98,10 @@
 def start(tokens, cotangent, gain):
     return pl.pallas_call(
         start_kernel,
+        grid=(1,),
         out_shape=shape(8, D),
-        in_specs=[VMEM] * 3,
-        out_specs=VMEM,
+        in_specs=[pl.BlockSpec((rows, D), lambda at: (0, 0)) for rows in (4, 4, 1)],
+        out_specs=pl.BlockSpec((8, D), lambda at: (0, 0)),
         compiler_params=PARAMS,
     )(tokens, cotangent, gain)
 
@@ -167,7 +168,7 @@
 
 def first_kernel(*refs):
     place, n_parts, c_parts, weights = refs[0], refs[1:5], refs[5:9], refs[9:11]
-    n_out, c_out, qk_ref, vd_ref = refs[11:15]
+    n_out, c_out, qk_ref, send_ref = refs[11:15]
     n_all, c_all, wq, wo, sems = refs[15:]
     copies = []
 
@@ -190,7 +191,9 @@
     for at in range(4):
         span = slice(QUARTER * at, QUARTER * at + QUARTER)
         projected += times_rows(n_all[:, span], wq[:, span])
-    qk_ref[...] = projected[:, : 2 * cols]
+    queries = projected[:, : 2 * cols]
+    qk_ref[...] = queries
+    send_ref[:, : 2 * cols], send_ref[:, 2 * cols : 4 * cols] = two_parts(queries)
     for copy in c_in:
         copy.wait()
     wo_in.wait()
@@ -199,7 +202,8 @@
     for at in range(4):
         span = slice(QUARTER * at, QUARTER * at + QUARTER)
         d_context += times_rows(c_all[:, span], wo[:, span])
-    vd_ref[...] = jnp.concatenate([projected[:, 2 * cols :], d_context], 1).astype(BF16)
+    values = projected[:, 2 * cols :]
+    send_ref[:, 4 * cols :] = jnp.concatenate([values, d_context], 1).astype(BF16)
     n_done.wait()
     c_done.wait()
 
@@ -212,7 +216,7 @@
             shape(ROWS, D),
             shape(ROWS, D),
             shape(ROWS, 2 * cols, dtype=F32),
-            shape(ROWS, 2 * cols),
+            shape(ROWS, 6 * cols),
         ],
         in_specs=[SMEM] + [ANY] * 10,
         out_specs=[ANY, ANY, VMEM, VMEM],
@@ -272,19 +276,17 @@
     )(n_all, c_all, w_in, w_out)
 
 
-def head_kernel(place, qk_own, qk_peer, vd_own, vd_peer, gains, ad, out, gain_ref):
+def head_kernel(place, qk_own, own, peer, gains, ad, out, gain_ref):
     cols = HD // 2
-
-    def whole(own, peer, left):
-        other = jnp.concatenate(
-            [peer[16 * (at ^ 1) : 16 * (at ^ 1) + 16, :] for at in range(ROWS // 16)], 0
-        )
-        return jnp.concatenate(
-            [own[:, left : left + cols], other[:, left : left + cols]], 1
-        )
-
-    query, key = whole(qk_own, qk_peer, 0), whole(qk_own, qk_peer, cols)
-    values, d_ctx = whole(vd_own, vd_peer, 0), whole(vd_own, vd_peer, cols)
+    other = jnp.concatenate(
+        [peer[16 * (at ^ 1) : 16 * (at ^ 1) + 16, :] for at in range(ROWS // 16)], 0
+    )
+    qk_other = other[:, :HD].astype(F32) + other[:, HD : 2 * HD].astype(F32)
+    query = jnp.concatenate([qk_own[:, :cols], qk_other[:, :cols]], 1)
+    key = jnp.concatenate([qk_own[:, cols:], qk_other[:, cols:]], 1)
+    left, right = slice(2 * HD, 2 * HD + cols), slice(2 * HD + cols, 3 * HD)
+    values = jnp.concatenate([own[:, left], other[:, left]], 1)
+    d_ctx = jnp.concatenate([own[:, right], other[:, right]], 1)
     q_gain, k_gain = gains[0:1, :], gains[1:2, :]
     q_scaled, q_inv = standardize(query)
     k_scaled, k_inv = standardize(key)
@@ -314,17 +316,17 @@
         gain_ref[row : row + 1, :] = jnp.where(place[2] == 0, even, odd)
 
 
-def head(place, qk_own, qk_peer, vd_own, vd_peer, gains, ad):
+def head(place, qk_own, own, peer, gains, ad):
     return pl.pallas_call(
         head_kernel,
         out_shape=[shape(ROWS, 2 * HD + ad.shape[1]), shape(2, HD, dtype=F32)],
-        in_specs=[SMEM] + [VMEM] * 6,
+        in_specs=[SMEM] + [VMEM] * 5,
         out_specs=[VMEM] * 2,
         compiler_params=PARAMS,
-    )(place, qk_own, qk_peer, vd_own, vd_peer, gains, ad)
-
-
-SLAB = 1024
+    )(place, qk_own, own, peer, gains, ad)
+
+
+SLAB = 1536
 STEPS = D // SLAB
 
 
@@ -668,14 +670,13 @@
     n_rows = join(n_parts)
     n_rows, c_rows, away = tie((n_rows, c_rows, away))
     n_parts, c_parts, there = tie((pieces(n_rows, Y), two_steps(c_rows), swapped(away, "dp", 2)))
-    n_all, c_all, qk_own, vd_own = first(place, n_parts, c_parts, w_flat, w_attn_out)
-
-    qk_peer, vd_peer = swapped(qk_own, "mp", X), swapped(vd_own, "mp", X)
-    there, n_next = tie((there, n_all))
     far = all_planes(there)
-    ad = hidden(n_next, c_all, w_mlp_in, w_mlp_out)
-    qk_peer, vd_peer, ad = tie((qk_peer, vd_peer, ad))
-    acts, gain_part = head(place, qk_own, qk_peer, vd_own, vd_peer, gains, ad)
+    n_all, c_all, qk_own, own = first(place, n_parts, c_parts, w_flat, w_attn_out)
+
+    peer = swapped(own, "mp", X)
+    ad = hidden(n_all, c_all, w_mlp_in, w_mlp_out)
+    peer, ad = tie((peer, ad))
+    acts, gain_part = head(place, qk_own, own, peer, gains, ad)
     outs = back(acts, w_attn_out, w_mlp_out, w_flat, w_mlp_in, n_all, gain_row, gain_part)
     kept, opposite, left, right, sums = outs[4:]
     left, right = swapped(left, "mp", X), swapped(right, "mp", 3 * X)

time: 218 us -> 215 us (0.986); the launches traced: 216 us -> 211 us
  waiting for transfers between devices: 86.5 us -> 82.3 us
  starting transfers between devices: 63.8 us -> 61.6 us
    ppermute x32 -> x31, waiting for transfers between devices: 86.3 us -> 82.1 us  [swapped(): lax.ppermute(block, axis, [(low, low ^ mask) for low in range(count)])]
    ppermute x32 -> x31, starting transfers between devices: 56.2 us -> 53.9 us  [swapped(): lax.ppermute(block, axis, [(low, low ^ mask) for low in range(count)])]
    unnamed x45 -> x49, local copies, waits for them, and re-layouts: 8.03 us -> 10.1 us
  transfers between devices with their start and end apart: 35 -> 34, of which waited for: 16 -> 19; matrix products, arithmetic and copies ran while one was open for 1% -> 1% of each run, Pallas kernels for 15% -> 18%
where the time goes in v1:
time: 215 us; the launch traced here: 211 us
  waiting for transfers between devices  82.3 us (38%)
  starting transfers between devices  61.6 us (29%)
  Pallas kernels  41 us (19%)
  between operations  14.3 us (7%)
  local copies, waits for them, and re-layouts  11.6 us (5%)
    ppermute x31, waiting for transfers between devices, swapped(): lax.ppermute(block, axis, [(low, low ^ mask) for low in range(count)])  82.1 us
    ppermute x31, starting transfers between devices, swapped(): lax.ppermute(block, axis, [(low, low ^ mask) for low in range(count)])  53.9 us
    unnamed x49, local copies, waits for them, and re-layouts  10.1 us
    pallas_call x1, Pallas kernels, back(): pl.pallas_call(back_kernel, grid=(STEPS,), out_shape=[shape(64, D)] * 6 +...  8.67 us
    all_to_all x2, starting transfers between devices, all_to_all(): lax.all_to_all(block, 'mp', 0, 0, axis_index_groups=groups, tiled=True)  7.68 us
    pallas_call x1, Pallas kernels, first(): pl.pallas_call(first_kernel, out_shape=[shape(ROWS, D), shape(ROWS, D), s...  7.32 us
    pallas_call x1, Pallas kernels, grads(): pl.pallas_call(grads_kernel, out_shape=[shape(height, QUARTER)] * 2, in_s...  6.83 us
    pallas_call x1, Pallas kernels, hidden(): pl.pallas_call(hidden_kernel, out_shape=shape(ROWS, 2 * units), in_specs=...  4.67 us
  transfers between devices with their start and end apart: 34, of which 19 were waited for; matrix products, arithmetic and copies ran while one was open for 1% of the time, Pallas kernels for 18%

profile of v1, /device:TPU:1, one launch (start us, length us, event | category | flops | bytes accessed | tf_op | source)
XLA Modules:
  0.0 210.7 jit_solution(13154817866601015865)
XLA Ops:
  9.8 5.3 %collective-permute-start.2 = (bf16[8,6144]{1,0:T(8,128)(2,1)S(1)}, bf16[8,6144]{1,0:T(8,128)(2,1)S(1)}, u32[]{:S(2)}, u32[]{:S(2)}) collective-permute-start(bf16[8,6144]{1,0:T(8,128)(2,1)S(1)} %shard_map.143.refs_0_), channel_id=1, source_target_pairs={{0,12},{1,13},{2,14},{3,15},{4,8},{5,9},{6,10},{7,11},{8,4},{9,5},... | collective-permute-start | bytes 294920 | tf_op jit(solution)/shard_map/ppermute | solution.py:31
  17.2 5.6 %collective-permute-done.1.refs_2_ = bf16[8,6144]{1,0:T(8,128)(2,1)S(1)} collective-permute-done((bf16[8,6144]{1,0:T(8,128)(2,1)S(1)}, bf16[8,6144]{1,0:T(8,128)(2,1)S(1)}, u32[]{:S(2)}, u32[]{:S(2)}) %collective-permute-start.1) | collective-permute-done | bytes 98336 | tf_op jit(solution)/shard_map/ppermute | solution.py:31
  24.5 4.2 %all-to-all-start = ((bf16[4,16,6144]{2,1,0:T(8,128)(2,1)}), bf16[4,16,6144]{2,1,0:T(8,128)(2,1)S(1)}, u32[]{:S(2)}, u32[]{:S(2)}) async-start(bf16[4,16,6144]{2,1,0:T(8,128)(2,1)} %bitcast.28), calls=%async_computation | async-start | bytes 1572864 | tf_op jit(solution)/shard_map/all_to_all | solution.py:641
  28.6 2.5 %collective-permute-start.5 = (bf16[16,6144]{1,0:T(8,128)(2,1)S(1)}, bf16[16,6144]{1,0:T(8,128)(2,1)S(1)}, u32[]{:S(2)}, u32[]{:S(2)}) collective-permute-start(bf16[16,6144]{1,0:T(8,128)(2,1)S(1)} %get-tuple-element.102.refs_0_), channel_id=1, source_target_pairs={{0,3},{1,2},{2,1},{3,0},{4,7},{5,6},{6,5},{7,4},{8,11},{9,10},{10,... | collective-permute-start | bytes 589832 | tf_op jit(solution)/shard_map/ppermute | solution.py:31
  31.9 7.4 %collective-permute-done.5.refs_3_ = bf16[16,6144]{1,0:T(8,128)(2,1)S(1)} collective-permute-done((bf16[16,6144]{1,0:T(8,128)(2,1)S(1)}, bf16[16,6144]{1,0:T(8,128)(2,1)S(1)}, u32[]{:S(2)}, u32[]{:S(2)}) %collective-permute-start.5) | collective-permute-done | bytes 196640 | tf_op jit(solution)/shard_map/ppermute | solution.py:31
  39.7 2.8 %collective-permute-start.9 = (bf16[64,6144]{1,0:T(8,128)(2,1)S(1)}, bf16[64,6144]{1,0:T(8,128)(2,1)S(1)}, u32[]{:S(2)}, u32[]{:S(2)}) collective-permute-start(bf16[64,6144]{1,0:T(8,128)(2,1)S(1)} %bitcast.35), channel_id=1, source_target_pairs={{0,2},{1,3},{2,0},{3,1},{4,6},{5,7},{6,4},{7,5},{8,10},{9,11},{10,... | collective-permute-start | bytes 2359304 | tf_op jit(solution)/shard_map/ppermute | solution.py:31
  45.8 5.6 %collective-permute-start.12 = (bf16[32,3072]{1,0:T(8,128)(2,1)S(1)}, bf16[32,3072]{1,0:T(8,128)(2,1)}, u32[]{:S(2)}, u32[]{:S(2)}) collective-permute-start(bf16[32,3072]{1,0:T(8,128)(2,1)S(1)} %get-tuple-element.110), channel_id=1, source_target_pairs={{0,128},{64,192},{128,0},{192,64},{1,129},{65,193},{129,1},{193,65... | collective-permute-start | bytes 589832 | tf_op jit(solution)/shard_map/ppermute | solution.py:31
  51.5 6.7 %collective-permute-done.9.refs_6_ = bf16[64,6144]{1,0:T(8,128)(2,1)S(1)} collective-permute-done((bf16[64,6144]{1,0:T(8,128)(2,1)S(1)}, bf16[64,6144]{1,0:T(8,128)(2,1)S(1)}, u32[]{:S(2)}, u32[]{:S(2)}) %collective-permute-start.9) | collective-permute-done | bytes 786464 | tf_op jit(solution)/shard_map/ppermute | solution.py:31
  59.5 3.8 %collective-permute-start.11 = (bf16[128,3072]{1,0:T(8,128)(2,1)}, bf16[128,3072]{1,0:T(8,128)(2,1)}, u32[]{:S(2)}, u32[]{:S(2)}) collective-permute-start(bf16[128,3072]{1,0:T(8,128)(2,1)} %get-tuple-element.184), channel_id=1, source_target_pairs={{0,3},{1,2},{2,1},{3,0},{4,7},{5,6},{6,5},{7,4},{8,11},{9,10},{10,... | collective-permute-start | bytes 2359304 | tf_op jit(solution)/shard_map/ppermute | solution.py:31
  63.3 15.0 %collective-permute-done.8.refs_4_ = bf16[64,6144]{1,0:T(8,128)(2,1)S(1)} collective-permute-done((bf16[64,6144]{1,0:T(8,128)(2,1)S(1)}, bf16[64,6144]{1,0:T(8,128)(2,1)S(1)}, u32[]{:S(2)}, u32[]{:S(2)}) %collective-permute-start.8) | collective-permute-done | bytes 786464 | tf_op jit(solution)/shard_map/ppermute | solution.py:31
  81.9 7.3 %shard_map.146 = (bf16[256,6144]{1,0:T(8,128)(2,1)}, bf16[256,6144]{1,0:T(8,128)(2,1)}, f32[256,128]{1,0:T(8,128)S(1)}, bf16[256,384]{1,0:T(8,128)(2,1)S(1)}) custom-call(s32[27]{0:T(128)S(1)} %stack.111.place.refs_0_, bf16[64,6144]{1,0:T(8,128)(2,1)S(1)} %shard_map.145.refs_1_, bf16[64,6144]{1,0:T(8,128)(2,1)} %collective-permute-done.6.refs_2_, ...), custom_call_target="tpu_custom_call" | custom-call | tf_op jit(solution)/shard_map/pallas_call | solution.py:213
  91.8 4.7 %shard_map.147.ad = bf16[256,512]{1,0:T(8,128)(2,1)S(1)} custom-call(bf16[256,6144]{1,0:T(8,128)(2,1)S(1)} %copy-done, bf16[256,6144]{1,0:T(8,128)(2,1)} %get-tuple-element.122.c_ref, bf16[256,6144]{1,0:T(8,128)(2,1)} %w_mi.1, bf16[256,6144]{1,0:T(8,128)(2,1)} %w_mo.1), custom_call_target="tpu_custom_call" | custom-call | tf_op jit(solution)/shard_map/pallas_call | solution.py:263
  96.5 2.4 %shard_map.148 = (bf16[256,768]{1,0:T(8,128)(2,1)S(1)}, f32[2,128]{1,0:T(2,128)S(1)}) custom-call(s32[27]{0:T(128)S(1)} %stack.111.place.refs_0_, f32[256,128]{1,0:T(8,128)S(1)} %get-tuple-element.119.qk_own, bf16[256,384]{1,0:T(8,128)(2,1)S(1)} %get-tuple-element.120.own, bf16[256,384]{1,0:T(8,128)(2,1)S(1)} %collective-permute-done.13.peer, ...), custom_call_target="tpu_custom_call" | custom-call | tf_op jit(solution)/shard_map/pallas_call | solution.py:320
  98.9 8.7 %shard_map.149 = (bf16[64,6144]{1,0:T(8,128)(2,1)S(1)}, bf16[64,6144]{1,0:T(8,128)(2,1)S(1)}, bf16[64,6144]{1,0:T(8,128)(2,1)}, bf16[64,6144]{1,0:T(8,128)(2,1)S...) custom-call(bf16[256,768]{1,0:T(8,128)(2,1)S(1)} %get-tuple-element., ...), custom_call_target="tpu_custom_call" | custom-call | tf_op jit(solution)/shard_map/pallas_call | solution.py:375
  114.1 5.2 %collective-permute-start.18 = (f32[64,128]{1,0:T(8,128)S(1)}, f32[64,128]{1,0:T(8,128)S(1)}, u32[]{:S(2)}, u32[]{:S(2)}) collective-permute-start(f32[64,128]{1,0:T(8,128)S(1)} %get-tuple-element.132.sums), channel_id=1, source_target_pairs={{0,64},{64,0},{128,192},{192,128},{1,65},{65,1},{129,193},{193,129... | collective-permute-start | bytes 98312 | tf_op jit(solution)/shard_map/ppermute | solution.py:31
  120.2 5.8 %collective-permute-start.19 = (bf16[288,768]{1,0:T(8,128)(2,1)S(1)}, bf16[288,768]{1,0:T(8,128)(2,1)S(1)}, u32[]{:S(2)}, u32[]{:S(2)}) collective-permute-start(bf16[288,768]{1,0:T(8,128)(2,1)S(1)} %shard_map.150.packed.acts), channel_id=1, source_target_pairs={{0,128},{64,192},{128,0},{192,64},{1,129},{65,193},{129,1},{193,65... | collective-permute-start | bytes 1327112 | tf_op jit(solution)/shard_map/ppermute | solution.py:31
  126.0 19.9 %collective-permute-done.19.packed_far.acts_far = bf16[288,768]{1,0:T(8,128)(2,1)S(1)} collective-permute-done((bf16[288,768]{1,0:T(8,128)(2,1)S(1)}, bf16[288,768]{1,0:T(8,128)(2,1)S(1)}, u32[]{:S(2)}, u32[]{:S(2)}) %collective-permute-start.19) | collective-permute-done | bytes 442400 | tf_op jit(solution)/shard_map/ppermute | solution.py:31
  150.0 6.8 %shard_map.152 = (bf16[768,1536]{1,0:T(8,128)(2,1)S(1)}, bf16[768,1536]{1,0:T(8,128)(2,1)}) custom-call(s32[27]{0:T(128)S(1)} %stack.111.place.refs_0_, bf16[288,768]{1,0:T(8,128)(2,1)S(1)} %shard_map.150.packed.acts, bf16[288,768]{1,0:T(8,128)(2,1)S(1)} %collective-permute-done.19.packed_far.acts_far, bf16[256,6144]{1,0:T(8,128)(2,1)} %get-tuple-element.121.n_ref, ...), custom_call_target="tpu_custom_call" | custom-call | tf_op jit(solution)/shard_map/pallas_call | solution.py:618
  158.3 6.9 %collective-permute-done.23.far = f32[64,128]{1,0:T(8,128)S(1)} collective-permute-done((f32[64,128]{1,0:T(8,128)S(1)}, f32[64,128]{1,0:T(8,128)S(1)}, u32[]{:S(2)}, u32[]{:S(2)}) %collective-permute-start.23) | collective-permute-done | bytes 32800 | tf_op jit(solution)/shard_map/ppermute | solution.py:31
  171.8 2.5 %shard_map.154 = bf16[64,6144]{1,0:T(8,128)(2,1)} custom-call(s32[27]{0:T(128)S(1)} %stack.111.place.refs_0_, bf16[64,6144]{1,0:T(8,128)(2,1)S(1)} %copy-done.5, bf16[64,6144]{1,0:T(8,128)(2,1)S(1)} %copy-done.9, bf16[64,6144]{1,0:T(8,128)(2,1)} %collective-permute-done.21.refs_2_, bf16[64,6144]{1,0:T(8,128)(2,1)S(1)} %copy-done.11), custom_call_target="tpu_custom_call" | custom-call | tf_op jit(solution)/shard_map/pallas_call | solution.py:481
  174.3 3.5 %all-to-all-start.1 = ((bf16[4,16,6144]{2,1,0:T(8,128)(2,1)}), bf16[4,16,6144]{2,1,0:T(8,128)(2,1)S(1)}, u32[]{:S(2)}, u32[]{:S(2)}) async-start(bf16[4,16,6144]{2,1,0:T(8,128)(2,1)} %bitcast.31), calls=%async_computation.1 | async-start | bytes 1572864 | tf_op jit(solution)/shard_map/all_to_all | solution.py:641
  181.8 3.4 %collective-permute-done.24.refs_2_ = bf16[16,7168]{1,0:T(8,128)(2,1)S(1)} collective-permute-done((bf16[16,7168]{1,0:T(8,128)(2,1)S(1)}, bf16[16,7168]{1,0:T(8,128)(2,1)S(1)}, u32[]{:S(2)}, u32[]{:S(2)}) %collective-permute-start.24) | collective-permute-done | bytes 229408 | tf_op jit(solution)/shard_map/ppermute | solution.py:31
  185.1 5.6 %collective-permute-done.25.refs_3_ = bf16[16,7168]{1,0:T(8,128)(2,1)S(1)} collective-permute-done((bf16[16,7168]{1,0:T(8,128)(2,1)S(1)}, bf16[16,7168]{1,0:T(8,128)(2,1)S(1)}, u32[]{:S(2)}, u32[]{:S(2)}) %collective-permute-start.25) | collective-permute-done | bytes 229408 | tf_op jit(solution)/shard_map/ppermute | solution.py:31
  196.8 3.6 %shard_map.156 = (bf16[192,1536]{1,0:T(8,128)(2,1)}, bf16[256,1536]{1,0:T(8,128)(2,1)}, bf16[64,1536]{1,0:T(8,128)(2,1)}, bf16[256,1536]{1,0:T(8,128)(2,1)}) custom-call(bf16[768,1536]{1,0:T(8,128)(2,1)} %copy-done.1, bf16[768,1536]{1,0:T(8,128)(2,1)} %collective-permute-done.30.taken), custom_call_target="tpu_custom_call" | custom-call | tf_op jit(solution)/shard_map/pallas_call | solution.py:564
  (114 shorter events, 51.6 us)
Async XLA Ops:
  24.5 15.2 %all-to-all-start = ((bf16[4,16,6144]{2,1,0:T(8,128)(2,1)}), bf16[4,16,6144]{2,1,0:T(8,128)(2,1)S(1)}, u32[]{:S(2)}, u32[]{:S(2)}) async-start(bf16[4,16,6144]{2,1,0:T(8,128)(2,1)} %bitcast.28), calls=%async_computation | async-start | bytes 1572864 | tf_op jit(solution)/shard_map/all_to_all | solution.py:641
  28.6 121.4 %all-gather.2.cloned.1.call-start = ((), (), s32[]{:S(2)}) async-start(), calls=%async_computation.2 | async-start | bytes 3342336 | tf_op jit(solution)/shard_map/all_gather | solution.py:646
  28.6 10.6 %collective-permute-start.5 = (bf16[16,6144]{1,0:T(8,128)(2,1)S(1)}, bf16[16,6144]{1,0:T(8,128)(2,1)S(1)}, u32[]{:S(2)}, u32[]{:S(2)}) collective-permute-start(bf16[16,6144]{1,0:T(8,128)(2,1)S(1)} %get-tuple-element.102.refs_0_), channel_id=1, source_target_pairs={{0,3},{1,2},{2,1},{3,0},{4,7},{5,6},{6,5},{7,4},{8,11},{9,10},{10,... | collective-permute-start | bytes 589832 | tf_op jit(solution)/shard_map/ppermute | solution.py:31
  31.1 8.1 %collective-permute-start.4 = (bf16[16,6144]{1,0:T(8,128)(2,1)S(1)}, bf16[16,6144]{1,0:T(8,128)(2,1)S(1)}, u32[]{:S(2)}, u32[]{:S(2)}) collective-permute-start(bf16[16,6144]{1,0:T(8,128)(2,1)S(1)} %get-tuple-element.102.refs_0_), channel_id=1, source_target_pairs={{0,2},{1,3},{2,0},{3,1},{4,6},{5,7},{6,4},{7,5},{8,10},{9,11},{10,... | collective-permute-start | bytes 589832 | tf_op jit(solution)/shard_map/ppermute | solution.py:31
  39.7 18.4 %collective-permute-start.9 = (bf16[64,6144]{1,0:T(8,128)(2,1)S(1)}, bf16[64,6144]{1,0:T(8,128)(2,1)S(1)}, u32[]{:S(2)}, u32[]{:S(2)}) collective-permute-start(bf16[64,6144]{1,0:T(8,128)(2,1)S(1)} %bitcast.35), channel_id=1, source_target_pairs={{0,2},{1,3},{2,0},{3,1},{4,6},{5,7},{6,4},{7,5},{8,10},{9,11},{10,... | collective-permute-start | bytes 2359304 | tf_op jit(solution)/shard_map/ppermute | solution.py:31
  42.6 35.7 %collective-permute-start.8 = (bf16[64,6144]{1,0:T(8,128)(2,1)S(1)}, bf16[64,6144]{1,0:T(8,128)(2,1)S(1)}, u32[]{:S(2)}, u32[]{:S(2)}) collective-permute-start(bf16[64,6144]{1,0:T(8,128)(2,1)S(1)} %shard_map.145.refs_1_), channel_id=1, source_target_pairs={{0,48},{1,49},{2,50},{3,51},{4,52},{5,53},{6,54},{7,55},{8,56},{9,... | collective-permute-start | bytes 2359304 | tf_op jit(solution)/shard_map/ppermute | solution.py:31
  44.9 33.4 %collective-permute-start.7 = (bf16[64,6144]{1,0:T(8,128)(2,1)S(1)}, bf16[64,6144]{1,0:T(8,128)(2,1)}, u32[]{:S(2)}, u32[]{:S(2)}) collective-permute-start(bf16[64,6144]{1,0:T(8,128)(2,1)S(1)} %shard_map.145.refs_1_), channel_id=1, source_target_pairs={{0,32},{1,33},{2,34},{3,35},{4,36},{5,37},{6,38},{7,39},{8,40},{9,... | collective-permute-start | bytes 2359304 | tf_op jit(solution)/shard_map/ppermute | solution.py:31
  45.4 32.8 %collective-permute-start.6 = (bf16[64,6144]{1,0:T(8,128)(2,1)S(1)}, bf16[64,6144]{1,0:T(8,128)(2,1)}, u32[]{:S(2)}, u32[]{:S(2)}) collective-permute-start(bf16[64,6144]{1,0:T(8,128)(2,1)S(1)} %shard_map.145.refs_1_), channel_id=1, source_target_pairs={{0,16},{1,17},{2,18},{3,19},{4,20},{5,21},{6,22},{7,23},{8,24},{9,... | collective-permute-start | bytes 2359304 | tf_op jit(solution)/shard_map/ppermute | solution.py:31
  45.8 17.4 %collective-permute-start.12 = (bf16[32,3072]{1,0:T(8,128)(2,1)S(1)}, bf16[32,3072]{1,0:T(8,128)(2,1)}, u32[]{:S(2)}, u32[]{:S(2)}) collective-permute-start(bf16[32,3072]{1,0:T(8,128)(2,1)S(1)} %get-tuple-element.110), channel_id=1, source_target_pairs={{0,128},{64,192},{128,0},{192,64},{1,129},{65,193},{129,1},{193,65... | collective-permute-start | bytes 589832 | tf_op jit(solution)/shard_map/ppermute | solution.py:31
  59.5 19.5 %collective-permute-start.11 = (bf16[128,3072]{1,0:T(8,128)(2,1)}, bf16[128,3072]{1,0:T(8,128)(2,1)}, u32[]{:S(2)}, u32[]{:S(2)}) collective-permute-start(bf16[128,3072]{1,0:T(8,128)(2,1)} %get-tuple-element.184), channel_id=1, source_target_pairs={{0,3},{1,2},{2,1},{3,0},{4,7},{5,6},{6,5},{7,4},{8,11},{9,10},{10,... | collective-permute-start | bytes 2359304 | tf_op jit(solution)/shard_map/ppermute | solution.py:31
  63.3 16.6 %collective-permute-start.10 = (bf16[128,3072]{1,0:T(8,128)(2,1)}, bf16[128,3072]{1,0:T(8,128)(2,1)S(1)}, u32[]{:S(2)}, u32[]{:S(2)}) collective-permute-start(bf16[128,3072]{1,0:T(8,128)(2,1)} %get-tuple-element.185), channel_id=1, source_target_pairs={{0,1},{1,0},{2,3},{3,2},{4,5},{5,4},{6,7},{7,6},{8,9},{9,8},{10,11... | collective-permute-start | bytes 2359304 | tf_op jit(solution)/shard_map/ppermute | solution.py:31
  108.5 37.3 %collective-permute-start.14 = (bf16[128,3072]{1,0:T(8,128)(2,1)S(1)}, bf16[128,3072]{1,0:T(8,128)(2,1)S(1)}, u32[]{:S(2)}, u32[]{:S(2)}) collective-permute-start(bf16[128,3072]{1,0:T(8,128)(2,1)S(1)} %get-tuple-element.128), channel_id=1, source_target_pairs={{0,1},{1,0},{2,3},{3,2},{4,5},{5,4},{6,7},{7,6},{8,9},{9,8},{10,11... | collective-permute-start | bytes 2359304 | tf_op jit(solution)/shard_map/ppermute | solution.py:31
  109.8 36.1 %collective-permute-start.15 = (bf16[128,3072]{1,0:T(8,128)(2,1)}, bf16[128,3072]{1,0:T(8,128)(2,1)S(1)}, u32[]{:S(2)}, u32[]{:S(2)}) collective-permute-start(bf16[128,3072]{1,0:T(8,128)(2,1)} %get-tuple-element.129), channel_id=1, source_target_pairs={{0,3},{1,2},{2,1},{3,0},{4,7},{5,6},{6,5},{7,4},{8,11},{9,10},{10,... | collective-permute-start | bytes 2359304 | tf_op jit(solution)/shard_map/ppermute | solution.py:31
  111.3 34.6 %collective-permute-start.16 = (bf16[64,6144]{1,0:T(8,128)(2,1)S(1)}, bf16[64,6144]{1,0:T(8,128)(2,1)S(1)}, u32[]{:S(2)}, u32[]{:S(2)}) collective-permute-start(bf16[64,6144]{1,0:T(8,128)(2,1)S(1)} %get-tuple-element.130), channel_id=1, source_target_pairs={{0,16},{1,17},{2,18},{3,19},{4,20},{5,21},{6,22},{7,23},{8,24},{9,... | collective-permute-start | bytes 2359304 | tf_op jit(solution)/shard_map/ppermute | solution.py:31
  112.3 33.5 %collective-permute-start.17 = (bf16[64,6144]{1,0:T(8,128)(2,1)S(1)}, bf16[64,6144]{1,0:T(8,128)(2,1)S(1)}, u32[]{:S(2)}, u32[]{:S(2)}) collective-permute-start(bf16[64,6144]{1,0:T(8,128)(2,1)S(1)} %get-tuple-element.131), channel_id=1, source_target_pairs={{0,48},{1,49},{2,50},{3,51},{4,52},{5,53},{6,54},{7,55},{8,56},{9,... | collective-permute-start | bytes 2359304 | tf_op jit(solution)/shard_map/ppermute | solution.py:31
  120.2 25.7 %collective-permute-start.19 = (bf16[288,768]{1,0:T(8,128)(2,1)S(1)}, bf16[288,768]{1,0:T(8,128)(2,1)S(1)}, u32[]{:S(2)}, u32[]{:S(2)}) collective-permute-start(bf16[288,768]{1,0:T(8,128)(2,1)S(1)} %shard_map.150.packed.acts), channel_id=1, source_target_pairs={{0,128},{64,192},{128,0},{192,64},{1,129},{65,193},{129,1},{193,65... | collective-permute-start | bytes 1327112 | tf_op jit(solution)/shard_map/ppermute | solution.py:31
  147.3 20.7 %collective-permute-start.20 = (bf16[64,6400]{1,0:T(8,128)(2,1)}, bf16[64,6400]{1,0:T(8,128)(2,1)S(1)}, u32[]{:S(2)}, u32[]{:S(2)}) collective-permute-start(bf16[64,6400]{1,0:T(8,128)(2,1)} %get-tuple-element.141), channel_id=1, source_target_pairs={{0,2},{1,3},{2,0},{3,1},{4,6},{5,7},{6,4},{7,5},{8,10},{9,11},{10,... | collective-permute-start | bytes 2457608 | tf_op jit(solution)/shard_map/ppermute | solution.py:31
  147.3 19.3 %collective-permute-start.21 = (bf16[64,6144]{1,0:T(8,128)(2,1)}, bf16[64,6144]{1,0:T(8,128)(2,1)}, u32[]{:S(2)}, u32[]{:S(2)}) collective-permute-start(bf16[64,6144]{1,0:T(8,128)(2,1)} %get-tuple-element.142), channel_id=1, source_target_pairs={{0,32},{1,33},{2,34},{3,35},{4,36},{5,37},{6,38},{7,39},{8,40},{9,... | collective-permute-start | bytes 2359304 | tf_op jit(solution)/shard_map/ppermute | solution.py:31
  147.4 17.7 %collective-permute-start.23 = (f32[64,128]{1,0:T(8,128)S(1)}, f32[64,128]{1,0:T(8,128)S(1)}, u32[]{:S(2)}, u32[]{:S(2)}) collective-permute-start(f32[64,128]{1,0:T(8,128)S(1)} %get-tuple-element.143.sums), channel_id=1, source_target_pairs={{0,3},{1,2},{2,1},{3,0},{4,7},{5,6},{6,5},{7,4},{8,11},{9,10},{10,... | collective-permute-start | bytes 98312 | tf_op jit(solution)/shard_map/ppermute | solution.py:31
  148.9 17.5 %collective-permute-start.22 = (f32[64,128]{1,0:T(8,128)S(1)}, f32[64,128]{1,0:T(8,128)S(1)}, u32[]{:S(2)}, u32[]{:S(2)}) collective-permute-start(f32[64,128]{1,0:T(8,128)S(1)} %get-tuple-element.143.sums), channel_id=1, source_target_pairs={{0,1},{1,0},{2,3},{3,2},{4,5},{5,4},{6,7},{7,6},{8,9},{9,8},{10,11... | collective-permute-start | bytes 98312 | tf_op jit(solution)/shard_map/ppermute | solution.py:31
  168.0 28.9 %collective-permute-start.30 = (bf16[768,1536]{1,0:T(8,128)(2,1)}, bf16[768,1536]{1,0:T(8,128)(2,1)}, u32[]{:S(2)}, u32[]{:S(2)}) collective-permute-start(bf16[768,1536]{1,0:T(8,128)(2,1)} %get-tuple-element.167), channel_id=1, source_target_pairs={{0,64},{64,0},{128,192},{192,128},{1,65},{65,1},{129,193},{193,129... | collective-permute-start | bytes 7077896 | tf_op jit(solution)/shard_map/ppermute | solution.py:31
  174.3 18.6 %all-to-all-start.1 = ((bf16[4,16,6144]{2,1,0:T(8,128)(2,1)}), bf16[4,16,6144]{2,1,0:T(8,128)(2,1)S(1)}, u32[]{:S(2)}, u32[]{:S(2)}) async-start(bf16[4,16,6144]{2,1,0:T(8,128)(2,1)} %bitcast.31), calls=%async_computation.1 | async-start | bytes 1572864 | tf_op jit(solution)/shard_map/all_to_all | solution.py:641
  178.3 12.4 %collective-permute-start.25 = (bf16[16,7168]{1,0:T(8,128)(2,1)S(1)}, bf16[16,7168]{1,0:T(8,128)(2,1)S(1)}, u32[]{:S(2)}, u32[]{:S(2)}) collective-permute-start(bf16[16,7168]{1,0:T(8,128)(2,1)S(1)} %copy-done.20), channel_id=1, source_target_pairs={{0,32},{1,33},{2,34},{3,35},{4,36},{5,37},{6,38},{7,39},{8,40},{9,... | collective-permute-start | bytes 688136 | tf_op jit(solution)/shard_map/ppermute | solution.py:31
  180.0 12.9 %collective-permute-start.26 = (bf16[16,7168]{1,0:T(8,128)(2,1)}, bf16[16,7168]{1,0:T(8,128)(2,1)S(1)}, u32[]{:S(2)}, u32[]{:S(2)}) collective-permute-start(bf16[16,7168]{1,0:T(8,128)(2,1)} %copy-done.18), channel_id=1, source_target_pairs={{0,48},{1,49},{2,50},{3,51},{4,52},{5,53},{6,54},{7,55},{8,56},{9,... | collective-permute-start | bytes 688136 | tf_op jit(solution)/shard_map/ppermute | solution.py:31
  (34 other events, 229.7 us)
Sparse Core Ops, SparseCore 0:
  80.9 63.9 all-gather.1

commit v2 on v1

--- a/solution.py
+++ b/solution.py
@@ -470,26 +470,25 @@
     )(*parts)
 
 
-def split_sum_kernel(place, *refs):
+def split_sum_kernel(*refs):
     for at in range(4):
         rows = slice(16 * at, 16 * at + 16)
-        spot = pl.ds(pl.multiple_of(place[19 + at], 16), 16)
-        refs[4][spot, :] = total([ref[rows, :] for ref in refs[:4]]).astype(BF16)
-
-
-def split_sum(place, parts):
+        refs[4 + at][...] = total([ref[rows, :] for ref in refs[:4]]).astype(BF16)
+
+
+def split_sum(parts):
     return pl.pallas_call(
         split_sum_kernel,
-        out_shape=shape(64, D),
-        in_specs=[SMEM] + [VMEM] * 4,
-        out_specs=VMEM,
-        compiler_params=PARAMS,
-    )(place, *parts)
+        out_shape=[shape(16, D)] * 4,
+        in_specs=[VMEM] * 4,
+        out_specs=[VMEM] * 4,
+        compiler_params=PARAMS,
+    )(*parts)
 
 
 def ends_kernel(*refs):
-    mixed_ref, back_refs, outs = refs[0], refs[1:5], refs[5:]
-    mixed = total([mixed_ref[16 * at : 16 * at + 16, :] for at in range(4)])
+    mixed_refs, back_refs, outs = refs[:4], refs[4:8], refs[8:]
+    mixed = total([ref[...] for ref in mixed_refs])
     back = total([ref[:, :D] for ref in back_refs])
     for at in range(4):
         rows = slice(4 * at, 4 * at + 4)
@@ -506,14 +505,14 @@
                 out[:, edge + 1024 : edge + 1152] = low
 
 
-def ends(mixed, back_parts):
+def ends(mixed_parts, back_parts):
     return pl.pallas_call(
         ends_kernel,
         out_shape=[shape(8, LAST_WIDE)] * 4,
-        in_specs=[VMEM] * 5,
+        in_specs=[VMEM] * 8,
         out_specs=[VMEM] * 4,
         compiler_params=PARAMS,
-    )(mixed, *back_parts)
+    )(*mixed_parts, *back_parts)
 
 
 def finish_kernel(first, second, third, fourth, tokens, cotangent, gain, out, d_out, ln_out, qk_out):
@@ -694,7 +693,7 @@
     spreads = spread(kept, left, right, got, sums, *other_sums)
     spreads, middle = tie((spreads, middle))
     back_parts = exchanged(spreads, Y)
-    mixed = all_to_all(split_sum(place, [outs[0], near, middle, late]), X)
+    mixed = exchanged(split_sum([outs[0], near, middle, late]), X)
     last = exchanged(ends(mixed, back_parts), Z)
     parts = add(keep, taken, (3 * cols, units, cols, units))
     last, parts = tie((last, parts))

time: 215 us -> 212 us (0.986)
    all_to_all x2 -> x1, starting transfers between devices: 7.68 us -> 4.18 us  [all_to_all(): lax.all_to_all(block, 'mp', 0, 0, axis_index_groups=groups, tiled=True)]
    ppermute x31 -> x34, starting transfers between devices: 53.9 us -> 56.9 us  [swapped(): lax.ppermute(block, axis, [(low, low ^ mask) for low in range(count)])]
    ppermute x31 -> x34, waiting for transfers between devices: 82.1 us -> 83.8 us  [swapped(): lax.ppermute(block, axis, [(low, low ^ mask) for low in range(count)])]
    unnamed x49 -> x39, local copies, waits for them, and re-layouts: 10.1 us -> 8.69 us
  transfers between devices with their start and end apart: 34 -> 36, of which waited for: 19 -> 20; matrix products, arithmetic and copies ran while one was open for 1% -> 1% of each run, Pallas kernels for 18% -> 18%
where the time goes in v2:
time: 212 us; the launch traced here: 210 us
  waiting for transfers between devices  83.9 us (40%)
  starting transfers between devices  61.1 us (29%)
  Pallas kernels  40.3 us (19%)
  between operations  14.3 us (7%)
  local copies, waits for them, and re-layouts  10.2 us (5%)
    ppermute x34, waiting for transfers between devices, swapped(): lax.ppermute(block, axis, [(low, low ^ mask) for low in range(count)])  83.8 us
    ppermute x34, starting transfers between devices, swapped(): lax.ppermute(block, axis, [(low, low ^ mask) for low in range(count)])  56.9 us
    unnamed x39, local copies, waits for them, and re-layouts  8.69 us
    pallas_call x1, Pallas kernels, back(): pl.pallas_call(back_kernel, grid=(STEPS,), out_shape=[shape(64, D)] * 6 +...  8.67 us
    pallas_call x1, Pallas kernels, first(): pl.pallas_call(first_kernel, out_shape=[shape(ROWS, D), shape(ROWS, D), s...  7.32 us
    pallas_call x1, Pallas kernels, grads(): pl.pallas_call(grads_kernel, out_shape=[shape(height, QUARTER)] * 2, in_s...  7.18 us
    pallas_call x1, Pallas kernels, hidden(): pl.pallas_call(hidden_kernel, out_shape=shape(ROWS, 2 * units), in_specs=...  4.67 us
  transfers between devices with their start and end apart: 36, of which 20 were waited for; matrix products, arithmetic and copies ran while one was open for 1% of the time, Pallas kernels for 18%

profile of v2, /device:TPU:1, one launch (start us, length us, event | category | flops | bytes accessed | tf_op | source)
XLA Modules:
  0.0 209.8 jit_solution(4906786797718431327)
XLA Ops:
  9.8 5.3 %collective-permute-start.2 = (bf16[8,6144]{1,0:T(8,128)(2,1)S(1)}, bf16[8,6144]{1,0:T(8,128)(2,1)S(1)}, u32[]{:S(2)}, u32[]{:S(2)}) collective-permute-start(bf16[8,6144]{1,0:T(8,128)(2,1)S(1)} %shard_map.143.refs_0_), channel_id=1, source_target_pairs={{0,12},{1,13},{2,14},{3,15},{4,8},{5,9},{6,10},{7,11},{8,4},{9,5},... | collective-permute-start | bytes 294920 | tf_op jit(solution)/shard_map/ppermute | solution.py:31
  17.2 5.6 %collective-permute-done.1.refs_2_ = bf16[8,6144]{1,0:T(8,128)(2,1)S(1)} collective-permute-done((bf16[8,6144]{1,0:T(8,128)(2,1)S(1)}, bf16[8,6144]{1,0:T(8,128)(2,1)S(1)}, u32[]{:S(2)}, u32[]{:S(2)}) %collective-permute-start.1) | collective-permute-done | bytes 98336 | tf_op jit(solution)/shard_map/ppermute | solution.py:31
  24.5 4.2 %all-to-all-start = ((bf16[4,16,6144]{2,1,0:T(8,128)(2,1)}), bf16[4,16,6144]{2,1,0:T(8,128)(2,1)S(1)}, u32[]{:S(2)}, u32[]{:S(2)}) async-start(bf16[4,16,6144]{2,1,0:T(8,128)(2,1)} %bitcast.28), calls=%async_computation | async-start | bytes 1572864 | tf_op jit(solution)/shard_map/all_to_all | solution.py:640
  28.6 2.5 %collective-permute-start.5 = (bf16[16,6144]{1,0:T(8,128)(2,1)S(1)}, bf16[16,6144]{1,0:T(8,128)(2,1)S(1)}, u32[]{:S(2)}, u32[]{:S(2)}) collective-permute-start(bf16[16,6144]{1,0:T(8,128)(2,1)S(1)} %get-tuple-element.106.refs_0_), channel_id=1, source_target_pairs={{0,3},{1,2},{2,1},{3,0},{4,7},{5,6},{6,5},{7,4},{8,11},{9,10},{10,... | collective-permute-start | bytes 589832 | tf_op jit(solution)/shard_map/ppermute | solution.py:31
  31.9 7.4 %collective-permute-done.5.refs_3_ = bf16[16,6144]{1,0:T(8,128)(2,1)S(1)} collective-permute-done((bf16[16,6144]{1,0:T(8,128)(2,1)S(1)}, bf16[16,6144]{1,0:T(8,128)(2,1)S(1)}, u32[]{:S(2)}, u32[]{:S(2)}) %collective-permute-start.5) | collective-permute-done | bytes 196640 | tf_op jit(solution)/shard_map/ppermute | solution.py:31
  39.7 2.8 %collective-permute-start.9 = (bf16[64,6144]{1,0:T(8,128)(2,1)S(1)}, bf16[64,6144]{1,0:T(8,128)(2,1)S(1)}, u32[]{:S(2)}, u32[]{:S(2)}) collective-permute-start(bf16[64,6144]{1,0:T(8,128)(2,1)S(1)} %bitcast.33), channel_id=1, source_target_pairs={{0,2},{1,3},{2,0},{3,1},{4,6},{5,7},{6,4},{7,5},{8,10},{9,11},{10,... | collective-permute-start | bytes 2359304 | tf_op jit(solution)/shard_map/ppermute | solution.py:31
  42.6 2.3 %collective-permute-start.8 = (bf16[64,6144]{1,0:T(8,128)(2,1)S(1)}, bf16[64,6144]{1,0:T(8,128)(2,1)S(1)}, u32[]{:S(2)}, u32[]{:S(2)}) collective-permute-start(bf16[64,6144]{1,0:T(8,128)(2,1)S(1)} %shard_map.145.refs_1_), channel_id=1, source_target_pairs={{0,48},{1,49},{2,50},{3,51},{4,52},{5,53},{6,54},{7,55},{8,56},{9,... | collective-permute-start | bytes 2359304 | tf_op jit(solution)/shard_map/ppermute | solution.py:31
  45.8 5.6 %collective-permute-start.12 = (bf16[32,3072]{1,0:T(8,128)(2,1)S(1)}, bf16[32,3072]{1,0:T(8,128)(2,1)}, u32[]{:S(2)}, u32[]{:S(2)}) collective-permute-start(bf16[32,3072]{1,0:T(8,128)(2,1)S(1)} %get-tuple-element.114), channel_id=1, source_target_pairs={{0,128},{64,192},{128,0},{192,64},{1,129},{65,193},{129,1},{193,65... | collective-permute-start | bytes 589832 | tf_op jit(solution)/shard_map/ppermute | solution.py:31
  51.5 6.7 %collective-permute-done.9.refs_6_ = bf16[64,6144]{1,0:T(8,128)(2,1)S(1)} collective-permute-done((bf16[64,6144]{1,0:T(8,128)(2,1)S(1)}, bf16[64,6144]{1,0:T(8,128)(2,1)S(1)}, u32[]{:S(2)}, u32[]{:S(2)}) %collective-permute-start.9) | collective-permute-done | bytes 786464 | tf_op jit(solution)/shard_map/ppermute | solution.py:31
  59.5 3.8 %collective-permute-start.11 = (bf16[128,3072]{1,0:T(8,128)(2,1)}, bf16[128,3072]{1,0:T(8,128)(2,1)}, u32[]{:S(2)}, u32[]{:S(2)}) collective-permute-start(bf16[128,3072]{1,0:T(8,128)(2,1)} %get-tuple-element.192), channel_id=1, source_target_pairs={{0,3},{1,2},{2,1},{3,0},{4,7},{5,6},{6,5},{7,4},{8,11},{9,10},{10,... | collective-permute-start | bytes 2359304 | tf_op jit(solution)/shard_map/ppermute | solution.py:31
  63.3 15.0 %collective-permute-done.8.refs_4_ = bf16[64,6144]{1,0:T(8,128)(2,1)S(1)} collective-permute-done((bf16[64,6144]{1,0:T(8,128)(2,1)S(1)}, bf16[64,6144]{1,0:T(8,128)(2,1)S(1)}, u32[]{:S(2)}, u32[]{:S(2)}) %collective-permute-start.8) | collective-permute-done | bytes 786464 | tf_op jit(solution)/shard_map/ppermute | solution.py:31
  81.9 7.3 %shard_map.146 = (bf16[256,6144]{1,0:T(8,128)(2,1)}, bf16[256,6144]{1,0:T(8,128)(2,1)}, f32[256,128]{1,0:T(8,128)S(1)}, bf16[256,384]{1,0:T(8,128)(2,1)S(1)}) custom-call(s32[27]{0:T(128)S(1)} %stack.111.place.refs_0_, bf16[64,6144]{1,0:T(8,128)(2,1)S(1)} %shard_map.145.refs_1_, bf16[64,6144]{1,0:T(8,128)(2,1)} %collective-permute-done.6.refs_2_, ...), custom_call_target="tpu_custom_call" | custom-call | tf_op jit(solution)/shard_map/pallas_call | solution.py:213
  91.8 4.7 %shard_map.147.ad = bf16[256,512]{1,0:T(8,128)(2,1)S(1)} custom-call(bf16[256,6144]{1,0:T(8,128)(2,1)S(1)} %copy-done, bf16[256,6144]{1,0:T(8,128)(2,1)} %get-tuple-element.126.c_ref, bf16[256,6144]{1,0:T(8,128)(2,1)} %w_mi.1, bf16[256,6144]{1,0:T(8,128)(2,1)} %w_mo.1), custom_call_target="tpu_custom_call" | custom-call | tf_op jit(solution)/shard_map/pallas_call | solution.py:263
  96.5 2.4 %shard_map.148 = (bf16[256,768]{1,0:T(8,128)(2,1)S(1)}, f32[2,128]{1,0:T(2,128)S(1)}) custom-call(s32[27]{0:T(128)S(1)} %stack.111.place.refs_0_, f32[256,128]{1,0:T(8,128)S(1)} %get-tuple-element.123.qk_own, bf16[256,384]{1,0:T(8,128)(2,1)S(1)} %get-tuple-element.124.own, bf16[256,384]{1,0:T(8,128)(2,1)S(1)} %collective-permute-done.13.peer, ...), custom_call_target="tpu_custom_call" | custom-call | tf_op jit(solution)/shard_map/pallas_call | solution.py:320
  98.9 8.7 %shard_map.149 = (bf16[64,6144]{1,0:T(8,128)(2,1)S(1)}, bf16[64,6144]{1,0:T(8,128)(2,1)S(1)}, bf16[64,6144]{1,0:T(8,128)(2,1)}, bf16[64,6144]{1,0:T(8,128)(2,1)S...) custom-call(bf16[256,768]{1,0:T(8,128)(2,1)S(1)} %get-tuple-element., ...), custom_call_target="tpu_custom_call" | custom-call | tf_op jit(solution)/shard_map/pallas_call | solution.py:375
  114.0 5.2 %collective-permute-start.18 = (f32[64,128]{1,0:T(8,128)S(1)}, f32[64,128]{1,0:T(8,128)S(1)}, u32[]{:S(2)}, u32[]{:S(2)}) collective-permute-start(f32[64,128]{1,0:T(8,128)S(1)} %get-tuple-element.136.sums), channel_id=1, source_target_pairs={{0,64},{64,0},{128,192},{192,128},{1,65},{65,1},{129,193},{193,129... | collective-permute-start | bytes 98312 | tf_op jit(solution)/shard_map/ppermute | solution.py:31
  120.1 5.8 %collective-permute-start.19 = (bf16[288,768]{1,0:T(8,128)(2,1)S(1)}, bf16[288,768]{1,0:T(8,128)(2,1)S(1)}, u32[]{:S(2)}, u32[]{:S(2)}) collective-permute-start(bf16[288,768]{1,0:T(8,128)(2,1)S(1)} %shard_map.150.packed.acts), channel_id=1, source_target_pairs={{0,128},{64,192},{128,0},{192,64},{1,129},{65,193},{129,1},{193,65... | collective-permute-start | bytes 1327112 | tf_op jit(solution)/shard_map/ppermute | solution.py:31
  125.9 19.9 %collective-permute-done.19.packed_far.acts_far = bf16[288,768]{1,0:T(8,128)(2,1)S(1)} collective-permute-done((bf16[288,768]{1,0:T(8,128)(2,1)S(1)}, bf16[288,768]{1,0:T(8,128)(2,1)S(1)}, u32[]{:S(2)}, u32[]{:S(2)}) %collective-permute-start.19) | collective-permute-done | bytes 442400 | tf_op jit(solution)/shard_map/ppermute | solution.py:31
  150.0 7.2 %shard_map.152 = (bf16[768,1536]{1,0:T(8,128)(2,1)S(1)}, bf16[768,1536]{1,0:T(8,128)(2,1)S(1)}) custom-call(s32[27]{0:T(128)S(1)} %stack.111.place.refs_0_, bf16[288,768]{1,0:T(8,128)(2,1)S(1)} %shard_map.150.packed.acts, bf16[288,768]{1,0:T(8,128)(2,1)S(1)} %collective-permute-done.19.packed_far.acts_far, bf16[256,6144]{1,0:T(8,128)(2,1)} %get-tuple-element.125.n_ref, ...), custom_call_target="tpu_custom_call" | custom-call | tf_op jit(solution)/shard_map/pallas_call | solution.py:617
  158.6 6.5 %collective-permute-done.23.far = f32[64,128]{1,0:T(8,128)S(1)} collective-permute-done((f32[64,128]{1,0:T(8,128)S(1)}, f32[64,128]{1,0:T(8,128)S(1)}, u32[]{:S(2)}, u32[]{:S(2)}) %collective-permute-start.23) | collective-permute-done | bytes 32800 | tf_op jit(solution)/shard_map/ppermute | solution.py:31
  179.4 4.1 %collective-permute-done.25.refs_2_ = bf16[16,6144]{1,0:T(8,128)(2,1)S(1)} collective-permute-done((bf16[16,6144]{1,0:T(8,128)(2,1)S(1)}, bf16[16,6144]{1,0:T(8,128)(2,1)S(1)}, u32[]{:S(2)}, u32[]{:S(2)}) %collective-permute-start.25) | collective-permute-done | bytes 196640 | tf_op jit(solution)/shard_map/ppermute | solution.py:31
  185.1 5.2 %collective-permute-done.26.refs_3_ = bf16[16,6144]{1,0:T(8,128)(2,1)S(1)} collective-permute-done((bf16[16,6144]{1,0:T(8,128)(2,1)S(1)}, bf16[16,6144]{1,0:T(8,128)(2,1)S(1)}, u32[]{:S(2)}, u32[]{:S(2)}) %collective-permute-start.26) | collective-permute-done | bytes 196640 | tf_op jit(solution)/shard_map/ppermute | solution.py:31
  194.9 3.6 %shard_map.156 = (bf16[192,1536]{1,0:T(8,128)(2,1)}, bf16[256,1536]{1,0:T(8,128)(2,1)}, bf16[64,1536]{1,0:T(8,128)(2,1)}, bf16[256,1536]{1,0:T(8,128)(2,1)}) custom-call(bf16[768,1536]{1,0:T(8,128)(2,1)} %copy-done.1, bf16[768,1536]{1,0:T(8,128)(2,1)} %collective-permute-done.33.taken), custom_call_target="tpu_custom_call" | custom-call | tf_op jit(solution)/shard_map/pallas_call | solution.py:563
  198.5 3.3 %collective-permute-done.32.fourth = bf16[8,8192]{1,0:T(8,128)(2,1)S(1)} collective-permute-done((bf16[8,8192]{1,0:T(8,128)(2,1)S(1)}, bf16[8,8192]{1,0:T(8,128)(2,1)S(1)}, u32[]{:S(2)}, u32[]{:S(2)}) %collective-permute-start.32) | collective-permute-done | bytes 131104 | tf_op jit(solution)/shard_map/ppermute | solution.py:31
  (108 shorter events, 50.7 us)
Async XLA Ops:
  24.5 15.2 %all-to-all-start = ((bf16[4,16,6144]{2,1,0:T(8,128)(2,1)}), bf16[4,16,6144]{2,1,0:T(8,128)(2,1)S(1)}, u32[]{:S(2)}, u32[]{:S(2)}) async-start(bf16[4,16,6144]{2,1,0:T(8,128)(2,1)} %bitcast.28), calls=%async_computation | async-start | bytes 1572864 | tf_op jit(solution)/shard_map/all_to_all | solution.py:640
  28.6 121.3 %all-gather.2.cloned.1.call-start = ((), (), s32[]{:S(2)}) async-start(), calls=%async_computation.1 | async-start | bytes 3342336 | tf_op jit(solution)/shard_map/all_gather | solution.py:645
  28.6 10.6 %collective-permute-start.5 = (bf16[16,6144]{1,0:T(8,128)(2,1)S(1)}, bf16[16,6144]{1,0:T(8,128)(2,1)S(1)}, u32[]{:S(2)}, u32[]{:S(2)}) collective-permute-start(bf16[16,6144]{1,0:T(8,128)(2,1)S(1)} %get-tuple-element.106.refs_0_), channel_id=1, source_target_pairs={{0,3},{1,2},{2,1},{3,0},{4,7},{5,6},{6,5},{7,4},{8,11},{9,10},{10,... | collective-permute-start | bytes 589832 | tf_op jit(solution)/shard_map/ppermute | solution.py:31
  39.7 18.4 %collective-permute-start.9 = (bf16[64,6144]{1,0:T(8,128)(2,1)S(1)}, bf16[64,6144]{1,0:T(8,128)(2,1)S(1)}, u32[]{:S(2)}, u32[]{:S(2)}) collective-permute-start(bf16[64,6144]{1,0:T(8,128)(2,1)S(1)} %bitcast.33), channel_id=1, source_target_pairs={{0,2},{1,3},{2,0},{3,1},{4,6},{5,7},{6,4},{7,5},{8,10},{9,11},{10,... | collective-permute-start | bytes 2359304 | tf_op jit(solution)/shard_map/ppermute | solution.py:31
  42.6 35.7 %collective-permute-start.8 = (bf16[64,6144]{1,0:T(8,128)(2,1)S(1)}, bf16[64,6144]{1,0:T(8,128)(2,1)S(1)}, u32[]{:S(2)}, u32[]{:S(2)}) collective-permute-start(bf16[64,6144]{1,0:T(8,128)(2,1)S(1)} %shard_map.145.refs_1_), channel_id=1, source_target_pairs={{0,48},{1,49},{2,50},{3,51},{4,52},{5,53},{6,54},{7,55},{8,56},{9,... | collective-permute-start | bytes 2359304 | tf_op jit(solution)/shard_map/ppermute | solution.py:31
  44.9 33.4 %collective-permute-start.7 = (bf16[64,6144]{1,0:T(8,128)(2,1)S(1)}, bf16[64,6144]{1,0:T(8,128)(2,1)}, u32[]{:S(2)}, u32[]{:S(2)}) collective-permute-start(bf16[64,6144]{1,0:T(8,128)(2,1)S(1)} %shard_map.145.refs_1_), channel_id=1, source_target_pairs={{0,32},{1,33},{2,34},{3,35},{4,36},{5,37},{6,38},{7,39},{8,40},{9,... | collective-permute-start | bytes 2359304 | tf_op jit(solution)/shard_map/ppermute | solution.py:31
  45.4 32.8 %collective-permute-start.6 = (bf16[64,6144]{1,0:T(8,128)(2,1)S(1)}, bf16[64,6144]{1,0:T(8,128)(2,1)}, u32[]{:S(2)}, u32[]{:S(2)}) collective-permute-start(bf16[64,6144]{1,0:T(8,128)(2,1)S(1)} %shard_map.145.refs_1_), channel_id=1, source_target_pairs={{0,16},{1,17},{2,18},{3,19},{4,20},{5,21},{6,22},{7,23},{8,24},{9,... | collective-permute-start | bytes 2359304 | tf_op jit(solution)/shard_map/ppermute | solution.py:31
  45.8 17.4 %collective-permute-start.12 = (bf16[32,3072]{1,0:T(8,128)(2,1)S(1)}, bf16[32,3072]{1,0:T(8,128)(2,1)}, u32[]{:S(2)}, u32[]{:S(2)}) collective-permute-start(bf16[32,3072]{1,0:T(8,128)(2,1)S(1)} %get-tuple-element.114), channel_id=1, source_target_pairs={{0,128},{64,192},{128,0},{192,64},{1,129},{65,193},{129,1},{193,65... | collective-permute-start | bytes 589832 | tf_op jit(solution)/shard_map/ppermute | solution.py:31
  59.5 19.5 %collective-permute-start.11 = (bf16[128,3072]{1,0:T(8,128)(2,1)}, bf16[128,3072]{1,0:T(8,128)(2,1)}, u32[]{:S(2)}, u32[]{:S(2)}) collective-permute-start(bf16[128,3072]{1,0:T(8,128)(2,1)} %get-tuple-element.192), channel_id=1, source_target_pairs={{0,3},{1,2},{2,1},{3,0},{4,7},{5,6},{6,5},{7,4},{8,11},{9,10},{10,... | collective-permute-start | bytes 2359304 | tf_op jit(solution)/shard_map/ppermute | solution.py:31
  63.3 16.6 %collective-permute-start.10 = (bf16[128,3072]{1,0:T(8,128)(2,1)}, bf16[128,3072]{1,0:T(8,128)(2,1)S(1)}, u32[]{:S(2)}, u32[]{:S(2)}) collective-permute-start(bf16[128,3072]{1,0:T(8,128)(2,1)} %get-tuple-element.193), channel_id=1, source_target_pairs={{0,1},{1,0},{2,3},{3,2},{4,5},{5,4},{6,7},{7,6},{8,9},{9,8},{10,11... | collective-permute-start | bytes 2359304 | tf_op jit(solution)/shard_map/ppermute | solution.py:31
  108.5 37.3 %collective-permute-start.14 = (bf16[128,3072]{1,0:T(8,128)(2,1)S(1)}, bf16[128,3072]{1,0:T(8,128)(2,1)S(1)}, u32[]{:S(2)}, u32[]{:S(2)}) collective-permute-start(bf16[128,3072]{1,0:T(8,128)(2,1)S(1)} %get-tuple-element.132), channel_id=1, source_target_pairs={{0,1},{1,0},{2,3},{3,2},{4,5},{5,4},{6,7},{7,6},{8,9},{9,8},{10,11... | collective-permute-start | bytes 2359304 | tf_op jit(solution)/shard_map/ppermute | solution.py:31
  109.7 36.1 %collective-permute-start.15 = (bf16[128,3072]{1,0:T(8,128)(2,1)}, bf16[128,3072]{1,0:T(8,128)(2,1)S(1)}, u32[]{:S(2)}, u32[]{:S(2)}) collective-permute-start(bf16[128,3072]{1,0:T(8,128)(2,1)} %get-tuple-element.133), channel_id=1, source_target_pairs={{0,3},{1,2},{2,1},{3,0},{4,7},{5,6},{6,5},{7,4},{8,11},{9,10},{10,... | collective-permute-start | bytes 2359304 | tf_op jit(solution)/shard_map/ppermute | solution.py:31
  111.2 34.6 %collective-permute-start.16 = (bf16[64,6144]{1,0:T(8,128)(2,1)S(1)}, bf16[64,6144]{1,0:T(8,128)(2,1)S(1)}, u32[]{:S(2)}, u32[]{:S(2)}) collective-permute-start(bf16[64,6144]{1,0:T(8,128)(2,1)S(1)} %get-tuple-element.134), channel_id=1, source_target_pairs={{0,16},{1,17},{2,18},{3,19},{4,20},{5,21},{6,22},{7,23},{8,24},{9,... | collective-permute-start | bytes 2359304 | tf_op jit(solution)/shard_map/ppermute | solution.py:31
  112.3 33.5 %collective-permute-start.17 = (bf16[64,6144]{1,0:T(8,128)(2,1)S(1)}, bf16[64,6144]{1,0:T(8,128)(2,1)S(1)}, u32[]{:S(2)}, u32[]{:S(2)}) collective-permute-start(bf16[64,6144]{1,0:T(8,128)(2,1)S(1)} %get-tuple-element.135), channel_id=1, source_target_pairs={{0,48},{1,49},{2,50},{3,51},{4,52},{5,53},{6,54},{7,55},{8,56},{9,... | collective-permute-start | bytes 2359304 | tf_op jit(solution)/shard_map/ppermute | solution.py:31
  120.1 25.7 %collective-permute-start.19 = (bf16[288,768]{1,0:T(8,128)(2,1)S(1)}, bf16[288,768]{1,0:T(8,128)(2,1)S(1)}, u32[]{:S(2)}, u32[]{:S(2)}) collective-permute-start(bf16[288,768]{1,0:T(8,128)(2,1)S(1)} %shard_map.150.packed.acts), channel_id=1, source_target_pairs={{0,128},{64,192},{128,0},{192,64},{1,129},{65,193},{129,1},{193,65... | collective-permute-start | bytes 1327112 | tf_op jit(solution)/shard_map/ppermute | solution.py:31
  147.2 20.7 %collective-permute-start.20 = (bf16[64,6400]{1,0:T(8,128)(2,1)}, bf16[64,6400]{1,0:T(8,128)(2,1)S(1)}, u32[]{:S(2)}, u32[]{:S(2)}) collective-permute-start(bf16[64,6400]{1,0:T(8,128)(2,1)} %get-tuple-element.145), channel_id=1, source_target_pairs={{0,2},{1,3},{2,0},{3,1},{4,6},{5,7},{6,4},{7,5},{8,10},{9,11},{10,... | collective-permute-start | bytes 2457608 | tf_op jit(solution)/shard_map/ppermute | solution.py:31
  147.2 19.2 %collective-permute-start.21 = (bf16[64,6144]{1,0:T(8,128)(2,1)}, bf16[64,6144]{1,0:T(8,128)(2,1)}, u32[]{:S(2)}, u32[]{:S(2)}) collective-permute-start(bf16[64,6144]{1,0:T(8,128)(2,1)} %get-tuple-element.146), channel_id=1, source_target_pairs={{0,32},{1,33},{2,34},{3,35},{4,36},{5,37},{6,38},{7,39},{8,40},{9,... | collective-permute-start | bytes 2359304 | tf_op jit(solution)/shard_map/ppermute | solution.py:31
  147.3 17.7 %collective-permute-start.23 = (f32[64,128]{1,0:T(8,128)S(1)}, f32[64,128]{1,0:T(8,128)S(1)}, u32[]{:S(2)}, u32[]{:S(2)}) collective-permute-start(f32[64,128]{1,0:T(8,128)S(1)} %get-tuple-element.147.sums), channel_id=1, source_target_pairs={{0,3},{1,2},{2,1},{3,0},{4,7},{5,6},{6,5},{7,4},{8,11},{9,10},{10,... | collective-permute-start | bytes 98312 | tf_op jit(solution)/shard_map/ppermute | solution.py:31
  148.8 17.5 %collective-permute-start.22 = (f32[64,128]{1,0:T(8,128)S(1)}, f32[64,128]{1,0:T(8,128)S(1)}, u32[]{:S(2)}, u32[]{:S(2)}) collective-permute-start(f32[64,128]{1,0:T(8,128)S(1)} %get-tuple-element.147.sums), channel_id=1, source_target_pairs={{0,1},{1,0},{2,3},{3,2},{4,5},{5,4},{6,7},{7,6},{8,9},{9,8},{10,11... | collective-permute-start | bytes 98312 | tf_op jit(solution)/shard_map/ppermute | solution.py:31
  167.9 27.0 %collective-permute-start.33 = (bf16[768,1536]{1,0:T(8,128)(2,1)S(1)}, bf16[768,1536]{1,0:T(8,128)(2,1)}, u32[]{:S(2)}, u32[]{:S(2)}) collective-permute-start(bf16[768,1536]{1,0:T(8,128)(2,1)S(1)} %get-tuple-element.175), channel_id=1, source_target_pairs={{0,64},{64,0},{128,192},{192,128},{1,65},{65,1},{129,193},{193,129... | collective-permute-start | bytes 7077896 | tf_op jit(solution)/shard_map/ppermute | solution.py:31
  172.2 11.3 %collective-permute-start.25 = (bf16[16,6144]{1,0:T(8,128)(2,1)S(1)}, bf16[16,6144]{1,0:T(8,128)(2,1)S(1)}, u32[]{:S(2)}, u32[]{:S(2)}) collective-permute-start(bf16[16,6144]{1,0:T(8,128)(2,1)S(1)} %get-tuple-element.164), channel_id=1, source_target_pairs={{0,2},{1,3},{2,0},{3,1},{4,6},{5,7},{6,4},{7,5},{8,10},{9,11},{10,... | collective-permute-start | bytes 589832 | tf_op jit(solution)/shard_map/ppermute | solution.py:31
  174.2 16.1 %collective-permute-start.27 = (bf16[16,7168]{1,0:T(8,128)(2,1)S(1)}, bf16[16,7168]{1,0:T(8,128)(2,1)S(1)}, u32[]{:S(2)}, u32[]{:S(2)}) collective-permute-start(bf16[16,7168]{1,0:T(8,128)(2,1)S(1)} %get-tuple-element.167), channel_id=1, source_target_pairs={{0,16},{1,17},{2,18},{3,19},{4,20},{5,21},{6,22},{7,23},{8,24},{9,... | collective-permute-start | bytes 688136 | tf_op jit(solution)/shard_map/ppermute | solution.py:31
  174.6 15.7 %collective-permute-start.28 = (bf16[16,7168]{1,0:T(8,128)(2,1)S(1)}, bf16[16,7168]{1,0:T(8,128)(2,1)S(1)}, u32[]{:S(2)}, u32[]{:S(2)}) collective-permute-start(bf16[16,7168]{1,0:T(8,128)(2,1)S(1)} %get-tuple-element.168), channel_id=1, source_target_pairs={{0,32},{1,33},{2,34},{3,35},{4,36},{5,37},{6,38},{7,39},{8,40},{9,... | collective-permute-start | bytes 688136 | tf_op jit(solution)/shard_map/ppermute | solution.py:31
  178.5 12.5 %collective-permute-start.29 = (bf16[16,7168]{1,0:T(8,128)(2,1)S(1)}, bf16[16,7168]{1,0:T(8,128)(2,1)S(1)}, u32[]{:S(2)}, u32[]{:S(2)}) collective-permute-start(bf16[16,7168]{1,0:T(8,128)(2,1)S(1)} %get-tuple-element.169), channel_id=1, source_target_pairs={{0,48},{1,49},{2,50},{3,51},{4,52},{5,53},{6,54},{7,55},{8,56},{9,... | collective-permute-start | bytes 688136 | tf_op jit(solution)/shard_map/ppermute | solution.py:31
  (31 other events, 223.6 us)
Sparse Core Ops, SparseCore 0:
  80.9 63.9 all-gather.1
